TPU v7x, 32 devices: a whole 2x2x4 slice. The times are simulated.
32 devices in a mesh: dp: 8 (over z, x), seq: 4 (over y, core).
Axes of the slice: x: 2, y: 2, z: 4, core: 2. Of those that a mesh axis runs over, the one named last changes fastest.
Arguments:
- patches: bfloat16 [4, 8, 48, 1024], P(None, 'dp', None, 'seq'), may hold values from -6 to 6
- segments: int32 [4, 8, 1024], P(None, 'dp', 'seq'), may hold values from 0 to 4
- embed_in: float32 [48, 768], P(None, 'dp'), may hold values from -0.875 to 0.875
- pos_table: float32 [1024, 768], P(None, 'dp'), may hold values from -3 to 3
- attn_qkv: float32 [768, 2304], P('dp'), may hold values from -0.21875 to 0.21875
- attn_out: float32 [768, 768], P('dp'), may hold values from -0.875 to 0.875
- mlp_up: float32 [768, 3072], P('dp'), may hold values from -0.21875 to 0.21875
- mlp_down: float32 [3072, 768], P(None, 'dp'), may hold values from -0.109375 to 0.109375
- head_out: float32 [768, 96], P('dp'), may hold values from -0.109375 to 0.109375
- vectors: float32 [8, 768], P(None, 'dp'), may hold values from 0.5 to 1.5
- first_embed_in: float32 [48, 768], P(None, 'dp'), may hold values from -2.3841858e-06 to 2.3841858e-06
- first_pos_table: float32 [1024, 768], P(None, 'dp'), may hold values from -7.4505806e-08 to 7.4505806e-08
- first_attn_qkv: float32 [768, 2304], P('dp'), may hold values from -2.3841858e-06 to 2.3841858e-06
- first_attn_out: float32 [768, 768], P('dp'), may hold values from -2.3841858e-06 to 2.3841858e-06
- first_mlp_up: float32 [768, 3072], P('dp'), may hold values from -2.3841858e-06 to 2.3841858e-06
- first_mlp_down: float32 [3072, 768], P(None, 'dp'), may hold values from -2.3841858e-06 to 2.3841858e-06
- first_head_out: float32 [768, 96], P('dp'), may hold values from -2.3841858e-06 to 2.3841858e-06
- first_vectors: float32 [8, 768], P(None, 'dp'), may hold values from -9.536743e-06 to 9.536743e-06
- second_embed_in: float32 [48, 768], P(None, 'dp'), may hold values from 6.5906064e-13 to 2.6312307e-12
- second_pos_table: float32 [1024, 768], P(None, 'dp'), may hold values from 6.436139e-16 to 2.5695613e-15
- second_attn_qkv: float32 [768, 2304], P('dp'), may hold values from 6.5906064e-13 to 2.6312307e-12
- second_attn_out: float32 [768, 768], P('dp'), may hold values from 6.5906064e-13 to 2.6312307e-12
- second_mlp_up: float32 [768, 3072], P('dp'), may hold values from 6.5906064e-13 to 2.6312307e-12
- second_mlp_down: float32 [3072, 768], P(None, 'dp'), may hold values from 6.5906064e-13 to 2.6312307e-12
- second_head_out: float32 [768, 96], P('dp'), may hold values from 6.5906064e-13 to 2.6312307e-12
- second_vectors: float32 [8, 768], P(None, 'dp'), may hold values from 1.054497e-11 to 4.2099692e-11
Outputs:
- loss_bits: float32 [], replicated
- valid_dims: float32 [], replicated
- grad_norm: float32 [], replicated
- new_embed_in: float32 [48, 768], P(None, 'dp')
- new_pos_table: float32 [1024, 768], P(None, 'dp')
- new_attn_qkv: float32 [768, 2304], P('dp')
- new_attn_out: float32 [768, 768], P('dp')
- new_mlp_up: float32 [768, 3072], P('dp')
- new_mlp_down: float32 [3072, 768], P(None, 'dp')
- new_head_out: float32 [768, 96], P('dp')
- new_vectors: float32 [8, 768], P(None, 'dp')
- new_first_embed_in: float32 [48, 768], P(None, 'dp')
- new_first_pos_table: float32 [1024, 768], P(None, 'dp')
- new_first_attn_qkv: float32 [768, 2304], P('dp')
- new_first_attn_out: float32 [768, 768], P('dp')
- new_first_mlp_up: float32 [768, 3072], P('dp')
- new_first_mlp_down: float32 [3072, 768], P(None, 'dp')
- new_first_head_out: float32 [768, 96], P('dp')
- new_first_vectors: float32 [8, 768], P(None, 'dp')
- new_second_embed_in: float32 [48, 768], P(None, 'dp')
- new_second_pos_table: float32 [1024, 768], P(None, 'dp')
- new_second_attn_qkv: float32 [768, 2304], P('dp')
- new_second_attn_out: float32 [768, 768], P('dp')
- new_second_mlp_up: float32 [768, 3072], P('dp')
- new_second_mlp_down: float32 [3072, 768], P(None, 'dp')
- new_second_head_out: float32 [768, 96], P('dp')
- new_second_vectors: float32 [8, 768], P(None, 'dp')
All inputs are finite; a program needn't handle non-finite values.
Results may differ from a plain program's by a relative error of at most 0.0024.
The roundings to bfloat16 on the way count: a program that leaves them out, or rounds other values in their place, can miss the bound.
Values may be sent and summed in bfloat16 or wider, within the bound.
A program may use at most 192 MiB of HBM per device.

v0:
```python
import math

import jax
import jax.numpy as jnp
from jax import lax
from jax.sharding import PartitionSpec as P

HEADS = 12
PATCH = 48
STEP = 10


RATE = 0.02
VEC_RATE = 0.15
BETA_ONE = 0.9
BETA_TWO = 0.95
ADAM_EPS = 1e-08
DECAY = 0.1
CLIP_AT = 0.01
NORM_EPS = 1e-05


def shifted(value, axis, steps):
    count = lax.axis_size(axis)
    first, last = (max(0, -steps), min(count, count - steps))
    return lax.ppermute(value, axis, [(source, source + steps) for source in range(first, last)])


def layer_norm(hidden, gain, shift):
    mean = jnp.mean(hidden, -1, keepdims=True)
    centred = hidden - mean
    var = jnp.mean(centred * centred, -1, keepdims=True)
    rstd = lax.rsqrt(var + NORM_EPS)
    unit = centred * rstd
    return (unit * gain + shift, unit, rstd)


def norm_back(grad, unit, rstd, gain):
    dunit = grad * gain
    dhid = rstd * (
        dunit
        - jnp.mean(dunit, -1, keepdims=True)
        - unit * jnp.mean(dunit * unit, -1, keepdims=True)
    )
    return (dhid, jnp.sum(grad * unit, 0), jnp.sum(grad, 0))


def attn_scores(query, keys, allowed, scale):
    scores = jnp.einsum("rqhd,rkhd->rhqk", query, keys, preferred_element_type=jnp.float32) * scale
    return jnp.where(allowed[:, None], scores, -1e30)


def adamw(weight, first, second, grad, rate, decay):
    new_first = BETA_ONE * first + (1.0 - BETA_ONE) * grad
    new_second = BETA_TWO * second + (1.0 - BETA_TWO) * grad * grad
    first_hat = new_first / (1.0 - BETA_ONE**STEP)
    second_hat = new_second / (1.0 - BETA_TWO**STEP)
    return (
        weight - rate * (first_hat / (jnp.sqrt(second_hat) + ADAM_EPS) + decay * weight),
        new_first,
        new_second,
    )


def body(
    patches,
    segments,
    embed_in,
    pos_table,
    attn_qkv,
    attn_out,
    mlp_up,
    mlp_down,
    head_out,
    vectors,
    first_embed_in,
    first_pos_table,
    first_attn_qkv,
    first_attn_out,
    first_mlp_up,
    first_mlp_down,
    first_head_out,
    first_vectors,
    second_embed_in,
    second_pos_table,
    second_attn_qkv,
    second_attn_out,
    second_mlp_up,
    second_mlp_down,
    second_head_out,
    second_vectors,
):
    masters = (embed_in, pos_table, attn_qkv, attn_out, mlp_up, mlp_down, head_out, vectors)
    firsts = (
        first_embed_in,
        first_pos_table,
        first_attn_qkv,
        first_attn_out,
        first_mlp_up,
        first_mlp_down,
        first_head_out,
        first_vectors,
    )
    seconds = (
        second_embed_in,
        second_pos_table,
        second_attn_qkv,
        second_attn_out,
        second_mlp_up,
        second_mlp_down,
        second_head_out,
        second_vectors,
    )
    local_count = jnp.sum((segments > 0).astype(jnp.int32)).astype(jnp.float32) * PATCH
    full = (
        lax.all_gather(embed_in.astype(jnp.bfloat16), "dp", axis=1, tiled=True),
        lax.all_gather(pos_table.astype(jnp.bfloat16), "dp", axis=1, tiled=True),
        lax.all_gather(attn_qkv.astype(jnp.bfloat16), "dp", axis=0, tiled=True),
        lax.all_gather(attn_out.astype(jnp.bfloat16), "dp", axis=0, tiled=True),
        lax.all_gather(mlp_up.astype(jnp.bfloat16), "dp", axis=0, tiled=True),
        lax.all_gather(mlp_down.astype(jnp.bfloat16), "dp", axis=1, tiled=True),
        lax.all_gather(head_out.astype(jnp.bfloat16), "dp", axis=0, tiled=True),
        lax.all_gather(vectors.astype(jnp.bfloat16), "dp", axis=1, tiled=True),
    )
    w_embed, w_table, w_qkv, w_attn, w_up, w_down, w_head, w_vec = full
    gains = w_vec.astype(jnp.float32)
    row_seg = lax.all_gather(segments, "seq", axis=2, tiled=True)
    following = shifted(patches[:, :, :, :1], "seq", -1)
    group = segments.shape[2]
    start = lax.axis_index("seq") * group
    width = w_qkv.shape[0]
    head_dim = width // HEADS
    scale = float(head_dim) ** (-0.5)

    def layer_forward(patch, seg, rseg, nxt):
        rows = seg.shape[0]
        length = rseg.shape[1]
        tokens = jnp.swapaxes(patch, 1, 2)
        flat_x = tokens.reshape(-1, PATCH)
        qpos = start + jnp.arange(group)
        kpos = jnp.arange(length)
        same = rseg[:, None, :] == seg[:, :, None]
        offset = jnp.sum((same & (kpos[None, None, :] < qpos[None, :, None])).astype(jnp.int32), -1)
        allowed = same & (kpos[None, None, :] <= qpos[None, :, None])
        flat_off = offset.reshape(-1)
        h0 = jnp.dot(flat_x, w_embed, preferred_element_type=jnp.float32) + (gains[6] - 1.0)
        h0 = h0 + w_table[flat_off].astype(jnp.float32)
        normed, unit_one, rstd_one = layer_norm(h0, gains[0], gains[1] - 1.0)
        normed_b = normed.astype(jnp.bfloat16)
        qkv = jnp.dot(normed_b, w_qkv, preferred_element_type=jnp.float32).astype(jnp.bfloat16)
        qkv = qkv.reshape(rows, group, 3 * width)
        query = qkv[:, :, :width]
        keys, values = (
            lax.all_gather(qkv[:, :, width : 2 * width], "seq", axis=1, tiled=True),
            lax.all_gather(qkv[:, :, 2 * width :], "seq", axis=1, tiled=True),
        )
        query_h = query.reshape(rows, group, HEADS, head_dim)
        keys_h = keys.reshape(rows, length, HEADS, head_dim)
        values_h = values.reshape(rows, length, HEADS, head_dim)
        scores = attn_scores(query_h, keys_h, allowed, scale)
        top = jnp.max(scores, -1, keepdims=True)
        lse = top + jnp.log(jnp.sum(jnp.exp(scores - top), -1, keepdims=True))
        probs = jnp.exp(scores - lse).astype(jnp.bfloat16)
        attended = jnp.einsum(
            "rhqk,rkhd->rqhd", probs, values_h, preferred_element_type=jnp.float32
        )
        attended = attended.astype(jnp.bfloat16).reshape(-1, width)
        h1 = h0 + jnp.dot(attended, w_attn, preferred_element_type=jnp.float32) + (gains[7] - 1.0)
        mixed, unit_two, rstd_two = layer_norm(h1, gains[2], gains[3] - 1.0)
        mixed_b = mixed.astype(jnp.bfloat16)
        upper = jnp.dot(mixed_b, w_up, preferred_element_type=jnp.float32)
        hidden_b = jax.nn.gelu(upper).astype(jnp.bfloat16)
        h2 = h1 + jnp.dot(hidden_b, w_down, preferred_element_type=jnp.float32)
        final, unit_fin, rstd_fin = layer_norm(h2, gains[4], gains[5] - 1.0)
        final_b = final.astype(jnp.bfloat16)
        out = jnp.dot(final_b, w_head, preferred_element_type=jnp.float32)
        shift = out[:, :PATCH]
        alpha = out[:, PATCH:]
        later = jnp.concatenate([tokens[:, 1:, :], jnp.swapaxes(nxt, 1, 2)], axis=1).reshape(
            -1, PATCH
        )
        padded = jnp.concatenate([rseg, jnp.zeros((rows, 1), jnp.int32)], axis=1)
        seg_next = lax.dynamic_slice_in_dim(padded, start + 1, group, 1)
        pair = ((seg == seg_next) & (seg > 0)).astype(jnp.float32).reshape(-1, 1)
        first = ((seg > 0) & (offset == 0)).astype(jnp.float32).reshape(-1, 1)
        shrink = jnp.exp(-alpha)
        scaled = (later.astype(jnp.float32) - shift) * shrink
        flat_f = flat_x.astype(jnp.float32)
        term = jnp.sum(pair * (0.5 * scaled * scaled + alpha)) + jnp.sum(
            first * 0.5 * flat_f * flat_f
        )
        kept = (
            flat_x,
            flat_off,
            allowed,
            unit_one,
            rstd_one,
            normed_b,
            query_h,
            keys_h,
            values_h,
            qkv,
            lse,
            attended,
            unit_two,
            rstd_two,
            mixed_b,
            upper,
            hidden_b,
            unit_fin,
            rstd_fin,
            final_b,
            pair,
            scaled,
            shrink,
            seg,
            rseg,
        )
        return (term, kept)

    def layer_backward(kept):
        (
            flat_x,
            flat_off,
            allowed,
            unit_one,
            rstd_one,
            normed_b,
            query_h,
            keys_h,
            values_h,
            qkv,
            lse,
            attended,
            unit_two,
            rstd_two,
            mixed_b,
            upper,
            hidden_b,
            unit_fin,
            rstd_fin,
            final_b,
            pair,
            scaled,
            shrink,
            seg,
            rseg,
        ) = kept
        rows = query_h.shape[0]
        length = keys_h.shape[1]
        dout = jnp.concatenate([-pair * scaled * shrink, pair * (1.0 - scaled * scaled)], axis=1)
        dout = dout.astype(jnp.bfloat16)
        grad_head = jnp.einsum("nd,ne->de", final_b, dout, preferred_element_type=jnp.float32)
        dfinal = jnp.einsum("ne,de->nd", dout, w_head, preferred_element_type=jnp.float32)
        dh2, gain_fin, shift_fin = norm_back(dfinal, unit_fin, rstd_fin, gains[4])
        down_b = dh2.astype(jnp.bfloat16)
        grad_down = jnp.einsum("nf,nd->fd", hidden_b, down_b, preferred_element_type=jnp.float32)
        dhidden = jnp.einsum("nd,fd->nf", down_b, w_down, preferred_element_type=jnp.float32)
        _, gelu_back = jax.vjp(jax.nn.gelu, upper)
        dupper = gelu_back(dhidden)[0].astype(jnp.bfloat16)
        grad_up = jnp.einsum("nd,nf->df", mixed_b, dupper, preferred_element_type=jnp.float32)
        dmixed = jnp.einsum("nf,df->nd", dupper, w_up, preferred_element_type=jnp.float32)
        dnorm_two, gain_two, shift_two = norm_back(dmixed, unit_two, rstd_two, gains[2])
        dh1 = dh2 + dnorm_two
        grad_bias_out = jnp.sum(dh1, 0)
        dattn_b = dh1.astype(jnp.bfloat16)
        grad_attn = jnp.einsum("ni,nd->id", attended, dattn_b, preferred_element_type=jnp.float32)
        dattended = jnp.einsum("nd,id->ni", dattn_b, w_attn, preferred_element_type=jnp.float32)
        dattended = dattended.astype(jnp.bfloat16).reshape(rows, -1, HEADS, head_dim)
        keys_back, values_back = (keys_h, values_h)
        scores = attn_scores(query_h, keys_back, allowed, scale)
        probs = jnp.exp(scores - lse)
        dprobs = jnp.einsum(
            "rqhd,rkhd->rhqk", dattended, values_back, preferred_element_type=jnp.float32
        )
        delta = jnp.sum(dprobs * probs, -1, keepdims=True)
        dscores = (probs * (dprobs - delta)).astype(jnp.bfloat16)
        dquery = (
            jnp.einsum("rhqk,rkhd->rqhd", dscores, keys_back, preferred_element_type=jnp.float32)
            * scale
        )
        dkeys = (
            jnp.einsum("rhqk,rqhd->rkhd", dscores, query_h, preferred_element_type=jnp.float32)
            * scale
        )
        dvalues = jnp.einsum(
            "rhqk,rqhd->rkhd",
            probs.astype(jnp.bfloat16),
            dattended,
            preferred_element_type=jnp.float32,
        )
        dkeys, dvalues = (
            lax.psum_scatter(
                dkeys.reshape(rows, length, width), "seq", scatter_dimension=1, tiled=True
            ),
            lax.psum_scatter(
                dvalues.reshape(rows, length, width), "seq", scatter_dimension=1, tiled=True
            ),
        )
        dqkv = jnp.concatenate([dquery.reshape(rows, -1, width), dkeys, dvalues], axis=-1)
        dqkv = dqkv.astype(jnp.bfloat16).reshape(-1, 3 * width)
        grad_qkv = jnp.einsum("nd,ne->de", normed_b, dqkv, preferred_element_type=jnp.float32)
        dnormed = jnp.einsum("ne,de->nd", dqkv, w_qkv, preferred_element_type=jnp.float32)
        dnorm_one, gain_one, shift_one = norm_back(dnormed, unit_one, rstd_one, gains[0])
        dh0 = dh1 + dnorm_one
        grad_bias_in = jnp.sum(dh0, 0)
        grad_table = jax.ops.segment_sum(dh0, flat_off, num_segments=length)
        grad_embed = jnp.einsum(
            "nc,nd->cd", flat_x, dh0.astype(jnp.bfloat16), preferred_element_type=jnp.float32
        )
        grad_vec = jnp.stack(
            [
                gain_one,
                shift_one,
                gain_two,
                shift_two,
                gain_fin,
                shift_fin,
                grad_bias_in,
                grad_bias_out,
            ]
        )
        return (
            grad_embed,
            grad_table,
            grad_qkv,
            grad_attn,
            grad_up,
            grad_down,
            grad_head,
            grad_vec,
        )

    def micro_step(carry, item):
        sums, total = carry
        term, kept = layer_forward(item[0], item[1], item[2], item[3])
        grads = layer_backward(kept)
        return ((tuple((s + g for s, g in zip(sums, grads))), total + term), None)

    zeros = tuple((jnp.zeros(w.shape, jnp.float32) for w in full))
    (grads, total), _ = lax.scan(
        micro_step, (zeros, jnp.zeros((), jnp.float32)), (patches, segments, row_seg, following)
    )
    shards = (
        lax.psum_scatter(grads[0], "dp", scatter_dimension=1, tiled=True),
        lax.psum_scatter(grads[1], "dp", scatter_dimension=1, tiled=True),
        lax.psum_scatter(grads[2], "dp", scatter_dimension=0, tiled=True),
        lax.psum_scatter(grads[3], "dp", scatter_dimension=0, tiled=True),
        lax.psum_scatter(grads[4], "dp", scatter_dimension=0, tiled=True),
        lax.psum_scatter(grads[5], "dp", scatter_dimension=1, tiled=True),
        lax.psum_scatter(grads[6], "dp", scatter_dimension=0, tiled=True),
        lax.psum_scatter(grads[7], "dp", scatter_dimension=1, tiled=True),
    )
    summed = lax.psum(
        (
            shards[0],
            shards[1],
            shards[2],
            shards[3],
            shards[4],
            shards[5],
            shards[6],
            shards[7],
            total,
            local_count,
        ),
        "seq",
    )
    pieces = summed[:8]
    squares = sum((jnp.sum(p * p) for p in pieces))
    squares_all, loss_all, total_count = lax.psum((squares, summed[8], summed[9]), "dp")
    norm = jnp.sqrt(squares_all) / total_count
    clip = jnp.minimum(1.0, CLIP_AT / (norm + 1e-06))
    results = [
        adamw(
            masters[i],
            firsts[i],
            seconds[i],
            pieces[i] / total_count * clip,
            RATE if i < 7 else VEC_RATE,
            DECAY if i < 7 else 0.0,
        )
        for i in range(8)
    ]
    news = [r[0] for r in results]
    nfirst = [r[1] for r in results]
    nsecond = [r[2] for r in results]
    return (
        loss_all / math.log(2.0),
        total_count,
        norm,
        news[0],
        news[1],
        news[2],
        news[3],
        news[4],
        news[5],
        news[6],
        news[7],
        nfirst[0],
        nfirst[1],
        nfirst[2],
        nfirst[3],
        nfirst[4],
        nfirst[5],
        nfirst[6],
        nfirst[7],
        nsecond[0],
        nsecond[1],
        nsecond[2],
        nsecond[3],
        nsecond[4],
        nsecond[5],
        nsecond[6],
        nsecond[7],
    )


def solution(mesh):
    in_specs = (
        P(None, "dp", None, "seq"),
        P(None, "dp", "seq"),
        P(None, "dp"),
        P(None, "dp"),
        P("dp", None),
        P("dp", None),
        P("dp", None),
        P(None, "dp"),
        P("dp", None),
        P(None, "dp"),
        P(None, "dp"),
        P(None, "dp"),
        P("dp", None),
        P("dp", None),
        P("dp", None),
        P(None, "dp"),
        P("dp", None),
        P(None, "dp"),
        P(None, "dp"),
        P(None, "dp"),
        P("dp", None),
        P("dp", None),
        P("dp", None),
        P(None, "dp"),
        P("dp", None),
        P(None, "dp"),
    )
    out_specs = (
        P(),
        P(),
        P(),
        P(None, "dp"),
        P(None, "dp"),
        P("dp", None),
        P("dp", None),
        P("dp", None),
        P(None, "dp"),
        P("dp", None),
        P(None, "dp"),
        P(None, "dp"),
        P(None, "dp"),
        P("dp", None),
        P("dp", None),
        P("dp", None),
        P(None, "dp"),
        P("dp", None),
        P(None, "dp"),
        P(None, "dp"),
        P(None, "dp"),
        P("dp", None),
        P("dp", None),
        P("dp", None),
        P(None, "dp"),
        P("dp", None),
        P(None, "dp"),
    )
    return jax.shard_map(body, mesh=mesh, in_specs=in_specs, out_specs=out_specs, check_vma=False)
```

profile of v0, /device:TPU:0, one launch (start us, length us, event | category | flops | bytes accessed | tf_op | source)
XLA Modules:
  0.0 2089.6 jit_solution(7910901059649349191)
XLA Ops:
  16.3 27.9 %all-gather.1 = bf16[8,96,8]{1,2,0:T(8,128)(2,1)S(1)} all-gather(bf16[1,96,8]{1,2,0:T(8,128)(2,1)S(1)} %convert_bitcast_fusion.3), channel_id=1, replica_groups=mesh['dp'=8,'seq'=4] {'dp'}, dimensions={0}, use_global_device_ids=true | all-gather | bytes 13824 | tf_op jit(solution)/shard_map/all_gather | solution.py:123
  45.0 7.3 all_gather.43
  52.2 30.8 %all-gather = bf16[8,96,48]{1,2,0:T(8,128)(2,1)S(1)} all-gather(bf16[1,96,48]{1,2,0:T(8,128)(2,1)S(1)} %convert_bitcast_fusion.2), channel_id=1, replica_groups=mesh['dp'=8,'seq'=4] {'dp'}, dimensions={0}, use_global_device_ids=true | all-gather | bytes 82944 | tf_op jit(solution)/shard_map/all_gather | solution.py:116
  83.1 33.7 %all_gather.49 = bf16[768,96]{1,0:T(8,128)(2,1)} all-gather(bf16[96,96]{1,0:T(8,128)(2,1)S(1)} %convert_element_type.203), channel_id=1, replica_groups=mesh['dp'=8,'seq'=4] {'dp'}, dimensions={0}, use_global_device_ids=true | all-gather | bytes 165888 | tf_op jit(solution)/shard_map/all_gather | solution.py:122
  119.6 22.2 %all-gather.18.cloned.1.call-done = bf16[3072,768]{0,1:T(8,128)(2,1)} async-done(((bf16[3072,96]{0,1:T(8,128)(2,1)}), bf16[3072,768]{0,1:T(8,128)(2,1)}) %all-gather.18.cloned.1.call-update) | async-done | bytes 4718608 | tf_op jit(solution)/shard_map/all_gather | solution.py:121
  141.8 6.6 copy.116
  148.4 35.6 %all-gather.14.cloned.1.call-done = bf16[768,768]{1,0:T(8,128)(2,1)} async-done(((bf16[96,768]{1,0:T(8,128)(2,1)}), bf16[768,768]{1,0:T(8,128)(2,1)}) %all-gather.14.cloned.1.call-update) | async-done | bytes 1179664 | tf_op jit(solution)/shard_map/all_gather | solution.py:119
  184.0 66.6 %all-gather.12.cloned.1.call-done = bf16[768,2304]{1,0:T(8,128)(2,1)} async-done(((bf16[96,2304]{1,0:T(8,128)(2,1)}), bf16[768,2304]{1,0:T(8,128)(2,1)}) %all-gather.12.cloned.1.call-update) | async-done | bytes 3538960 | tf_op jit(solution)/shard_map/all_gather | solution.py:118
  250.6 81.0 %all-gather.16.cloned.1.call-done = bf16[768,3072]{1,0:T(8,128)(2,1)} async-done(((bf16[96,3072]{1,0:T(8,128)(2,1)}), bf16[768,3072]{1,0:T(8,128)(2,1)}) %all-gather.16.cloned.1.call-update) | async-done | bytes 4718608 | tf_op jit(solution)/shard_map/all_gather | solution.py:120
  333.5 796.1 %while.30 = (s32[]{:T(128)}, f32[48,768]{1,0:T(8,128)}, f32[1024,768]{1,0:T(8,128)}, f32[768,2304]{1,0:T(8,128)}, f32[768,768]{1,0:T(8,128)}, /*index=5*/f32[768...) while((s32[]{:T(128)}, f32[48,768]{1,0:T(8,128)}, ...), condition=%wide.region_30.31_spmd.clone, body=%wide.region_0.30_spmd.clone.sunk | while | flops 13596700672 | bytes 519567328 | solution.py:341
  349.1 15.0 all-gather.22.cloned.1.call-done
  373.2 12.9 all-gather.20.cloned.1.call-done
  388.6 8.1 convolution_convert_fusion.5
  404.4 15.5 fusion.203
  427.2 9.6 fusion.205
  436.9 8.1 multiply_reduce_fusion.33
  445.1 7.1 multiply_convert_fusion.11
  484.4 31.1 %reduce-scatter.33.cloned.1.call-done = f32[1,256,768]{1,2,0:T(8,128)} async-done(((f32[1,1024,768]{1,2,0:T(8,128)}), f32[1,256,768]{1,2,0:T(8,128)}) %reduce-scatter.33.cloned.1.call-update) | async-done | bytes 786448 | tf_op jit(solution)/shard_map/while/body/eval_jaxpr/reduce_scatter | solution.py:293
  522.1 6.1 scatter_fusion
  549.4 16.9 all-gather.22.cloned.1.call-done
  575.0 13.1 all-gather.20.cloned.1.call-done
  590.8 8.1 convolution_convert_fusion.5
  617.0 9.6 fusion.205
  626.7 8.1 multiply_reduce_fusion.33
  634.9 7.1 multiply_convert_fusion.11
  663.6 9.2 select_add_fusion.12
  672.8 8.2 select_add_fusion.13
  682.1 23.2 %reduce-scatter.33.cloned.1.call-done = f32[1,256,768]{1,2,0:T(8,128)} async-done(((f32[1,1024,768]{1,2,0:T(8,128)}), f32[1,256,768]{1,2,0:T(8,128)}) %reduce-scatter.33.cloned.1.call-update) | async-done | bytes 786448 | tf_op jit(solution)/shard_map/while/body/eval_jaxpr/reduce_scatter | solution.py:293
  712.1 6.3 scatter_fusion
  718.4 7.3 select_add_fusion.10
  742.2 17.0 all-gather.22.cloned.1.call-done
  768.0 12.9 all-gather.20.cloned.1.call-done
  783.6 8.1 convolution_convert_fusion.5
  810.0 9.6 fusion.205
  819.7 8.1 multiply_reduce_fusion.33
  827.9 7.1 multiply_convert_fusion.11
  856.6 9.2 select_add_fusion.12
  865.8 8.2 select_add_fusion.13
  875.1 22.9 %reduce-scatter.33.cloned.1.call-done = f32[1,256,768]{1,2,0:T(8,128)} async-done(((f32[1,1024,768]{1,2,0:T(8,128)}), f32[1,256,768]{1,2,0:T(8,128)}) %reduce-scatter.33.cloned.1.call-update) | async-done | bytes 786448 | tf_op jit(solution)/shard_map/while/body/eval_jaxpr/reduce_scatter | solution.py:293
  911.0 7.3 select_add_fusion.10
  934.9 16.9 all-gather.22.cloned.1.call-done
  960.7 13.0 all-gather.20.cloned.1.call-done
  976.3 8.1 convolution_convert_fusion.5
  992.1 15.4 fusion.203
  1014.7 9.6 fusion.205
  1024.4 8.1 multiply_reduce_fusion.33
  1032.6 7.1 multiply_convert_fusion.11
  1061.3 9.2 select_add_fusion.12
  1070.5 8.2 select_add_fusion.13
  1079.8 23.2 %reduce-scatter.33.cloned.1.call-done = f32[1,256,768]{1,2,0:T(8,128)} async-done(((f32[1,1024,768]{1,2,0:T(8,128)}), f32[1,256,768]{1,2,0:T(8,128)}) %reduce-scatter.33.cloned.1.call-update) | async-done | bytes 786448 | tf_op jit(solution)/shard_map/while/body/eval_jaxpr/reduce_scatter | solution.py:293
  1109.8 6.0 scatter_fusion
  1115.9 7.3 select_add_fusion.10
  1135.3 9.7 copy.118
  1149.6 53.3 %reduce-scatter.19.cloned.1.call-done = f32[96,768]{1,0:T(8,128)} async-done(((f32[768,768]{1,0:T(8,128)}), f32[96,768]{1,0:T(8,128)}) %reduce-scatter.19.cloned.1.call-update) | async-done | bytes 294928 | tf_op jit(solution)/shard_map/reduce_scatter | solution.py:348
  1202.9 77.0 %reduce-scatter.15.cloned.1.call-done = f32[1024,96]{0,1:T(8,128)} async-done(((f32[1024,768]{0,1:T(8,128)}), f32[1024,96]{0,1:T(8,128)}) %reduce-scatter.15.cloned.1.call-update) | async-done | bytes 393232 | tf_op jit(solution)/shard_map/reduce_scatter | solution.py:346
  1279.9 131.7 %reduce-scatter.17.cloned.1.call-done = f32[96,2304]{1,0:T(8,128)} async-done(((f32[768,2304]{1,0:T(8,128)}), f32[96,2304]{1,0:T(8,128)}) %reduce-scatter.17.cloned.1.call-update) | async-done | bytes 884752 | tf_op jit(solution)/shard_map/reduce_scatter | solution.py:347
  1411.6 166.6 %reduce-scatter.21.cloned.1.call-done = f32[96,3072]{1,0:T(8,128)} async-done(((f32[768,3072]{1,0:T(8,128)}), f32[96,3072]{1,0:T(8,128)}) %reduce-scatter.21.cloned.1.call-update) | async-done | bytes 1179664 | tf_op jit(solution)/shard_map/reduce_scatter | solution.py:349
  1578.2 166.5 %reduce-scatter.23.cloned.1.call-done = f32[3072,96]{0,1:T(8,128)} async-done(((f32[3072,768]{0,1:T(8,128)}), f32[3072,96]{0,1:T(8,128)}) %reduce-scatter.23.cloned.1.call-update) | async-done | bytes 1179664 | tf_op jit(solution)/shard_map/reduce_scatter | solution.py:350
  1746.8 62.4 %reduce-scatter.29.cloned.1.call-done = f32[96,8]{1,0:T(8,128)} async-done(((f32[768,8]{1,0:T(8,128)}), f32[96,8]{1,0:T(8,128)}) %reduce-scatter.29.cloned.1.call-update) | async-done | bytes 3088
  1810.1 63.8 %reduce-scatter.27.cloned.1.call-done = f32[96,48]{1,0:T(8,128)} async-done(((f32[768,48]{1,0:T(8,128)}), f32[96,48]{1,0:T(8,128)}) %reduce-scatter.27.cloned.1.call-update) | async-done | bytes 18448
  1874.7 63.8 %reduce-scatter.25.cloned.1.call-done = f32[96,96]{1,0:T(8,128)} async-done(((f32[768,96]{1,0:T(8,128)}), f32[96,96]{1,0:T(8,128)}) %reduce-scatter.25.cloned.1.call-update) | async-done | bytes 36880 | tf_op jit(solution)/shard_map/reduce_scatter | solution.py:351
  1938.5 13.2 all-reduce.1
  1953.5 69.0 %all-reduce.5.cloned.1.call-done = (f32[1024,96]{0,1:T(8,128)}, f32[96,2304]{1,0:T(8,128)}, f32[96,768]{1,0:T(8,128)}, f32[96,3072]{1,0:T(8,128)}, f32[3072,96]{0,1:T(8,128)}) async-done(((f32[1024,96]{0,1:T(8,128)}, f32[96,2304]{1,0:T(8,128)}, f32[96,768]{1,0:T(8,128)}, f32[96,3072]{1,0:T(8,128)}, f32[3072,96]{0,1:T(8,128)}), (f32[1024,96]{0,1:T(8,128)}, f32[96,2304]{1,0:T(8,128)}, f32[96,768]{1,0:T(8,128)}, ...) | async-done | bytes 3932176 | tf_op jit(solution)/shard_map/psum | solution.py:354
  2035.4 22.0 %all-reduce = (f32[]{:T(128)}, f32[]{:T(128)}, f32[]{:T(128)}) all-reduce(f32[]{:T(128)} %get-tuple-element.621, f32[]{:T(128)} %get-tuple-element.622, f32[]{:T(128)S(6)} %add.561), channel_id=1, replica_groups=mesh['dp'=8,'seq'=4] {'dp'}, use_global_device_ids=true, to_apply=%region_32.33 | all-reduce | flops 3 | bytes 24 | tf_op jit(solution)/shard_map/psum | solution.py:371
  (819 shorter events, 365.8 us)
Async XLA Ops:
  7.2 109.7 %all-gather.10.cloned.1.call-start = ((), (), s32[]{:S(2)}) async-start(), calls=%async_computation.10 | async-start | bytes 1769472 | tf_op jit(solution)/shard_map/all_gather | solution.py:117
  9.2 132.6 %all-gather.18.cloned.1.call-start = ((), (), s32[]{:S(2)}) async-start(), calls=%async_computation.14 | async-start | bytes 5308416 | tf_op jit(solution)/shard_map/all_gather | solution.py:121
  11.4 33.6 %copy-start.61 = (f32[96,96]{1,0:T(8,128)S(1)}, f32[96,96]{1,0:T(8,128)}, u32[]{:S(2)}) copy-start(f32[96,96]{1,0:T(8,128)} %param.36) | copy-start | bytes 110596
  11.4 40.8 %copy-start.63 = (f32[48,96]{1,0:T(8,128)S(1)}, f32[48,96]{1,0:T(8,128)}, u32[]{:S(2)}) copy-start(f32[48,96]{1,0:T(8,128)} %param.30) | copy-start | bytes 55300
  11.4 172.6 %all-gather.14.cloned.1.call-start = ((), (), s32[]{:S(2)}) async-start(), calls=%async_computation.12 | async-start | bytes 1327104 | tf_op jit(solution)/shard_map/all_gather | solution.py:119
  12.2 238.4 %all-gather.12.cloned.1.call-start = ((), (), s32[]{:S(2)}) async-start(), calls=%async_computation.11 | async-start | bytes 3981312 | tf_op jit(solution)/shard_map/all_gather | solution.py:118
  13.1 318.5 %all-gather.16.cloned.1.call-start = ((), (), s32[]{:S(2)}) async-start(), calls=%async_computation.13 | async-start | bytes 5308416 | tf_op jit(solution)/shard_map/all_gather | solution.py:120
  14.9 133.4 %collective-permute-start = (bf16[4,1,48,1]{2,3,1,0:T(2,128)(2,1)S(1)}, bf16[4,1,48,1]{2,3,1,0:T(2,128)(2,1)}, u32[]{:S(2)}, u32[]{:S(2)}) collective-permute-start(bf16[4,1,48,1]{2,3,1,0:T(2,128)(2,1)S(1)} %copy.124), channel_id=1, source_target_pairs={{1,0},{2,1},{3,2},{5,4},{6,5},{7,6},{9,8},{10,9},{11,10},{13,12},{... | collective-permute-start | bytes 1160 | tf_op jit(solution)/shard_map/ppermute | solution.py:26
  333.5 30.7 %all-gather.22.cloned.1.call-start = ((), (), s32[]{:S(2)}) async-start(), calls=%async_computation.25 | async-start | bytes 1966080 | tf_op jit(solution)/shard_map/while/body/eval_jaxpr/all_gather | solution.py:154
  335.6 13.1 copy-start.53
  346.1 39.9 %all-gather.20.cloned.1.call-start = ((), (), s32[]{:S(2)}) async-start(), calls=%async_computation.24 | async-start | bytes 1966080 | tf_op jit(solution)/shard_map/while/body/eval_jaxpr/all_gather | solution.py:155
  346.9 136.3 %reduce-scatter.31.cloned.1.call-start = ((), (), s32[]{:S(2)}) async-start(), calls=%async_computation.26 | async-start | bytes 3932160 | tf_op jit(solution)/shard_map/while/body/eval_jaxpr/reduce_scatter | solution.py:296
  348.7 19.9 copy-start.9
  397.4 24.8 %copy-start.47 = (f32[256]{0:T(256)}, f32[256]{0:T(256)S(1)}, u32[]{:S(2)}) copy-start(f32[256]{0:T(256)S(1)} %broadcast_multiply_fusion.18) | copy-start | bytes 3076 | tf_op jit(solution)/shard_map/while
  397.6 24.6 %copy-start.51 = (f32[256]{0:T(256)}, f32[256]{0:T(256)S(1)}, u32[]{:S(2)}) copy-start(f32[256]{0:T(256)S(1)} %add_rsqrt_fusion.7) | copy-start | bytes 3076 | tf_op jit(solution)/shard_map/while
  404.4 17.9 copy-start.7
  436.8 78.7 %reduce-scatter.33.cloned.1.call-start = ((), (), s32[]{:S(2)}) async-start(), calls=%async_computation.27 | async-start | bytes 3932160 | tf_op jit(solution)/shard_map/while/body/eval_jaxpr/reduce_scatter | solution.py:293
  478.1 38.6 %copy-start.46 = (f32[256]{0:T(256)S(1)}, f32[256]{0:T(256)}, u32[]{:S(2)}) copy-start(f32[256]{0:T(256)} %copy-done.45) | copy-start | bytes 3076 | tf_op jit(solution)/shard_map/while
  478.1 38.6 %copy-start.50 = (f32[256]{0:T(256)S(1)}, f32[256]{0:T(256)}, u32[]{:S(2)}) copy-start(f32[256]{0:T(256)} %copy-done.49) | copy-start | bytes 3076 | tf_op jit(solution)/shard_map/while
  533.7 32.6 %all-gather.22.cloned.1.call-start = ((), (), s32[]{:S(2)}) async-start(), calls=%async_computation.25 | async-start | bytes 1966080 | tf_op jit(solution)/shard_map/while/body/eval_jaxpr/all_gather | solution.py:154
  535.8 13.2 copy-start.53
  546.4 41.7 %all-gather.20.cloned.1.call-start = ((), (), s32[]{:S(2)}) async-start(), calls=%async_computation.24 | async-start | bytes 1966080 | tf_op jit(solution)/shard_map/while/body/eval_jaxpr/all_gather | solution.py:155
  547.2 133.8 %reduce-scatter.31.cloned.1.call-start = ((), (), s32[]{:S(2)}) async-start(), calls=%async_computation.26 | async-start | bytes 3932160 | tf_op jit(solution)/shard_map/while/body/eval_jaxpr/reduce_scatter | solution.py:296
  549.0 21.4 %copy-start.9 = (bf16[1,256,768]{1,2,0:T(8,128)(2,1)}, bf16[1,256,768]{1,2,0:T(8,128)(2,1)S(1)}, u32[]{:S(2)}) copy-start(bf16[1,256,768]{1,2,0:T(8,128)(2,1)S(1)} %copy.131) | copy-start | bytes 1179652 | tf_op jit(solution)/shard_map/while
  626.6 78.6 %reduce-scatter.33.cloned.1.call-start = ((), (), s32[]{:S(2)}) async-start(), calls=%async_computation.27 | async-start | bytes 3932160 | tf_op jit(solution)/shard_map/while/body/eval_jaxpr/reduce_scatter | solution.py:293
  672.7 33.7 %copy-start.46 = (f32[256]{0:T(256)S(1)}, f32[256]{0:T(256)}, u32[]{:S(2)}) copy-start(f32[256]{0:T(256)} %copy-done.45) | copy-start | bytes 3076 | tf_op jit(solution)/shard_map/while
  672.8 33.7 %copy-start.50 = (f32[256]{0:T(256)S(1)}, f32[256]{0:T(256)}, u32[]{:S(2)}) copy-start(f32[256]{0:T(256)} %copy-done.49) | copy-start | bytes 3076 | tf_op jit(solution)/shard_map/while
  726.6 32.6 %all-gather.22.cloned.1.call-start = ((), (), s32[]{:S(2)}) async-start(), calls=%async_computation.25 | async-start | bytes 1966080 | tf_op jit(solution)/shard_map/while/body/eval_jaxpr/all_gather | solution.py:154
  728.8 13.0 copy-start.53
  739.4 41.6 %all-gather.20.cloned.1.call-start = ((), (), s32[]{:S(2)}) async-start(), calls=%async_computation.24 | async-start | bytes 1966080 | tf_op jit(solution)/shard_map/while/body/eval_jaxpr/all_gather | solution.py:155
  740.0 134.0 %reduce-scatter.31.cloned.1.call-start = ((), (), s32[]{:S(2)}) async-start(), calls=%async_computation.26 | async-start | bytes 3932160 | tf_op jit(solution)/shard_map/while/body/eval_jaxpr/reduce_scatter | solution.py:296
  741.8 21.6 %copy-start.9 = (bf16[1,256,768]{1,2,0:T(8,128)(2,1)}, bf16[1,256,768]{1,2,0:T(8,128)(2,1)S(1)}, u32[]{:S(2)}) copy-start(bf16[1,256,768]{1,2,0:T(8,128)(2,1)S(1)} %copy.131) | copy-start | bytes 1179652 | tf_op jit(solution)/shard_map/while
  792.3 12.7 copy-start.47
  819.6 78.4 %reduce-scatter.33.cloned.1.call-start = ((), (), s32[]{:S(2)}) async-start(), calls=%async_computation.27 | async-start | bytes 3932160 | tf_op jit(solution)/shard_map/while/body/eval_jaxpr/reduce_scatter | solution.py:293
  865.8 33.5 %copy-start.46 = (f32[256]{0:T(256)S(1)}, f32[256]{0:T(256)}, u32[]{:S(2)}) copy-start(f32[256]{0:T(256)} %copy-done.45) | copy-start | bytes 3076 | tf_op jit(solution)/shard_map/while
  865.8 33.5 %copy-start.50 = (f32[256]{0:T(256)S(1)}, f32[256]{0:T(256)}, u32[]{:S(2)}) copy-start(f32[256]{0:T(256)} %copy-done.49) | copy-start | bytes 3076 | tf_op jit(solution)/shard_map/while
  919.3 32.6 %all-gather.22.cloned.1.call-start = ((), (), s32[]{:S(2)}) async-start(), calls=%async_computation.25 | async-start | bytes 1966080 | tf_op jit(solution)/shard_map/while/body/eval_jaxpr/all_gather | solution.py:154
  921.4 13.1 copy-start.53
  932.0 41.7 %all-gather.20.cloned.1.call-start = ((), (), s32[]{:S(2)}) async-start(), calls=%async_computation.24 | async-start | bytes 1966080 | tf_op jit(solution)/shard_map/while/body/eval_jaxpr/all_gather | solution.py:155
  932.8 145.9 %reduce-scatter.31.cloned.1.call-start = ((), (), s32[]{:S(2)}) async-start(), calls=%async_computation.26 | async-start | bytes 3932160 | tf_op jit(solution)/shard_map/while/body/eval_jaxpr/reduce_scatter | solution.py:296
  934.5 21.6 %copy-start.9 = (bf16[1,256,768]{1,2,0:T(8,128)(2,1)}, bf16[1,256,768]{1,2,0:T(8,128)(2,1)S(1)}, u32[]{:S(2)}) copy-start(bf16[1,256,768]{1,2,0:T(8,128)(2,1)S(1)} %copy.131) | copy-start | bytes 1179652 | tf_op jit(solution)/shard_map/while
  985.1 24.7 %copy-start.47 = (f32[256]{0:T(256)}, f32[256]{0:T(256)S(1)}, u32[]{:S(2)}) copy-start(f32[256]{0:T(256)S(1)} %broadcast_multiply_fusion.18) | copy-start | bytes 3076 | tf_op jit(solution)/shard_map/while
  985.3 24.4 %copy-start.51 = (f32[256]{0:T(256)}, f32[256]{0:T(256)S(1)}, u32[]{:S(2)}) copy-start(f32[256]{0:T(256)S(1)} %add_rsqrt_fusion.7) | copy-start | bytes 3076 | tf_op jit(solution)/shard_map/while
  992.1 17.7 copy-start.7
  1024.4 78.6 %reduce-scatter.33.cloned.1.call-start = ((), (), s32[]{:S(2)}) async-start(), calls=%async_computation.27 | async-start | bytes 3932160 | tf_op jit(solution)/shard_map/while/body/eval_jaxpr/reduce_scatter | solution.py:293
  1070.5 33.7 %copy-start.46 = (f32[256]{0:T(256)S(1)}, f32[256]{0:T(256)}, u32[]{:S(2)}) copy-start(f32[256]{0:T(256)} %copy-done.45) | copy-start | bytes 3076 | tf_op jit(solution)/shard_map/while
  1070.5 33.7 %copy-start.50 = (f32[256]{0:T(256)S(1)}, f32[256]{0:T(256)}, u32[]{:S(2)}) copy-start(f32[256]{0:T(256)} %copy-done.49) | copy-start | bytes 3076 | tf_op jit(solution)/shard_map/while
  1129.6 73.3 %reduce-scatter.19.cloned.1.call-start = ((), (), s32[]{:S(2)}) async-start(), calls=%async_computation.17 | async-start | bytes 2654208 | tf_op jit(solution)/shard_map/reduce_scatter | solution.py:348
  1130.3 149.6 %reduce-scatter.15.cloned.1.call-start = ((), (), s32[]{:S(2)}) async-start(), calls=%async_computation.15 | async-start | bytes 3538944 | tf_op jit(solution)/shard_map/reduce_scatter | solution.py:346
  1133.9 277.7 %reduce-scatter.17.cloned.1.call-start = ((), (), s32[]{:S(2)}) async-start(), calls=%async_computation.16 | async-start | bytes 7962624 | tf_op jit(solution)/shard_map/reduce_scatter | solution.py:347
  1134.5 443.7 %reduce-scatter.21.cloned.1.call-start = ((), (), s32[]{:S(2)}) async-start(), calls=%async_computation.18 | async-start | bytes 10616832 | tf_op jit(solution)/shard_map/reduce_scatter | solution.py:349
  1135.3 609.4 %reduce-scatter.23.cloned.1.call-start = ((), (), s32[]{:S(2)}) async-start(), calls=%async_computation.19 | async-start | bytes 10616832 | tf_op jit(solution)/shard_map/reduce_scatter | solution.py:350
  1145.0 664.2 %reduce-scatter.29.cloned.1.call-start = ((), (), s32[]{:S(2)}) async-start(), calls=%async_computation.22 | async-start | bytes 442368
  1146.6 727.2 %reduce-scatter.27.cloned.1.call-start = ((), (), s32[]{:S(2)}) async-start(), calls=%async_computation.21 | async-start | bytes 442368
  1148.6 789.9 %reduce-scatter.25.cloned.1.call-start = ((), (), s32[]{:S(2)}) async-start(), calls=%async_computation.20 | async-start | bytes 442368 | tf_op jit(solution)/shard_map/reduce_scatter | solution.py:351
  1149.6 872.9 %all-reduce.5.cloned.1.call-start = ((), (), s32[]{:S(2)}) async-start(), calls=%async_computation.23 | async-start | bytes 7864320 | tf_op jit(solution)/shard_map/psum | solution.py:354
  1744.7 314.8 %copy-start.66 = (f32[8,96]{1,0:T(8,128)S(1)}, f32[8,96]{1,0:T(8,128)}, u32[]{:S(2)}) copy-start(f32[8,96]{1,0:T(8,128)} %param.37) | copy-start | bytes 9220
  1744.7 314.8 %copy-start.67 = (f32[8,96]{1,0:T(8,128)S(1)}, f32[8,96]{1,0:T(8,128)}, u32[]{:S(2)}) copy-start(f32[8,96]{1,0:T(8,128)} %param.45) | copy-start | bytes 9220
  1744.7 314.8 %copy-start.68 = (f32[8,96]{1,0:T(8,128)S(1)}, f32[8,96]{1,0:T(8,128)}, u32[]{:S(2)}) copy-start(f32[8,96]{1,0:T(8,128)} %param.53) | copy-start | bytes 9220
  1744.7 320.5 %copy-start.38 = (f32[96,768]{1,0:T(8,128)S(1)}, f32[96,768]{1,0:T(8,128)}, u32[]{:S(2)}) copy-start(f32[96,768]{1,0:T(8,128)} %param.33) | copy-start | bytes 884740
  2022.5 42.7 %copy-start.39 = (f32[96,768]{1,0:T(8,128)S(1)}, f32[96,768]{1,0:T(8,128)}, u32[]{:S(2)}) copy-start(f32[96,768]{1,0:T(8,128)} %get-tuple-element.628) | copy-start | bytes 884740
  2022.5 45.4 %copy-start.31 = (f32[1024,96]{0,1:T(8,128)S(1)}, f32[1024,96]{0,1:T(8,128)}, u32[]{:S(2)}) copy-start(f32[1024,96]{0,1:T(8,128)} %param.31) | copy-start | bytes 1179652
  2022.5 45.4 %copy-start.55 = (f32[1024,96]{0,1:T(8,128)S(1)}, f32[1024,96]{0,1:T(8,128)}, u32[]{:S(2)}) copy-start(f32[1024,96]{0,1:T(8,128)} %param.39) | copy-start | bytes 1179652
  2028.7 42.1 %copy-start.26 = (f32[96,2304]{1,0:T(8,128)S(1)}, f32[96,2304]{1,0:T(8,128)}, u32[]{:S(2)}) copy-start(f32[96,2304]{1,0:T(8,128)} %param.32) | copy-start | bytes 2654212
  (169 other events, 810.5 us)
Sparse Core Ops, SparseCore 0:
  10.8 47.0 all-gather.9
  60.7 81.0 all-gather.17
  144.5 39.4 all-gather.13
  186.6 63.9 all-gather.11
  253.2 78.3 all-gather.15
  346.3 17.8 all-gather.21
  366.3 19.6 all-gather.19
  437.0 37.9 reduce-scatter.30
  477.5 37.9 reduce-scatter.32
  546.5 19.6 all-gather.21
  568.5 19.6 all-gather.19
  626.8 37.9 reduce-scatter.30
  667.3 37.9 reduce-scatter.32
  739.5 19.6 all-gather.21
  761.3 19.6 all-gather.19
  819.8 37.9 reduce-scatter.30
  860.1 37.8 reduce-scatter.32
  932.1 19.6 all-gather.21
  954.0 19.6 all-gather.19
  1024.5 37.9 reduce-scatter.30
  1065.0 37.9 reduce-scatter.32
  1133.9 68.9 reduce-scatter.18
  1206.5 73.3 reduce-scatter.14
  1283.4 128.1 reduce-scatter.16
  1415.6 162.5 reduce-scatter.20
  1582.0 162.5 reduce-scatter.22
  1748.7 60.4 reduce-scatter.28
  1813.4 60.4 reduce-scatter.26
  1878.0 60.3 reduce-scatter.24
  1941.2 81.2 all-reduce.4
where the time goes:
time: 2090 us
  waiting for transfers between devices  1280 us (61%)
  matrix products  357 us (17%)
  other arithmetic  146 us (7%)
  blocking collectives  135 us (6%)
  local copies, waits for them, and re-layouts  127 us (6%)
  between operations  25.1 us (1%)
    reduce_scatter x1, waiting for transfers between devices, body(): lax.psum_scatter(grads[4], 'dp', scatter_dimension=0, tiled=True)  167 us
    reduce_scatter x1, waiting for transfers between devices, body(): lax.psum_scatter(grads[5], 'dp', scatter_dimension=1, tiled=True)  167 us
    reduce_scatter x1, waiting for transfers between devices, body(): lax.psum_scatter(grads[2], 'dp', scatter_dimension=0, tiled=True)  132 us
    unnamed x16, waiting for transfers between devices  128 us
    reduce_scatter x4, waiting for transfers between devices, layer_backward(): lax.psum_scatter(dkeys.reshape(rows, length, width), 'seq', scatter_dimen...  100 us
    all_gather x1, waiting for transfers between devices, body(): lax.all_gather(mlp_up.astype(jnp.bfloat16), 'dp', axis=0, tiled=True)  81 us
    reduce_scatter x1, waiting for transfers between devices, body(): lax.psum_scatter(grads[1], 'dp', scatter_dimension=1, tiled=True)  77 us
    psum x1, waiting for transfers between devices, body(): lax.psum((shards[0], shards[1], shards[2], shards[3], shards[4], shards[5...  69 us
  transfers between devices with their start and end apart: 31, of which 25 were waited for; matrix products, arithmetic and copies ran while one was open for 14% of the time, Pallas kernels for 0%

commit v1 on v0

v1 whole, which is shorter than its diff:
```python
import functools
import math

import jax
import jax.numpy as jnp
from jax import lax
from jax.experimental import pallas as pl
from jax.experimental.pallas import tpu as pltpu
from jax.sharding import PartitionSpec as P

HEADS = 12
PATCH = 48
STEP = 10
RATE = 0.02
VEC_RATE = 0.15
BETA_ONE = 0.9
BETA_TWO = 0.95
ADAM_EPS = 1e-08
DECAY = 0.1
CLIP_AT = 0.01
NORM_EPS = 1e-05

F32 = jnp.float32
BF16 = jnp.bfloat16
WIRE = jnp.bfloat16
NN = (((1,), (0,)), ((), ()))
NT = (((1,), (1,)), ((), ()))
TN = (((0,), (0,)), ((), ()))


def dot(left, right, dims=NN):
    return lax.dot_general(left, right, dims, preferred_element_type=F32)


def line(axis, size, count, stride):
    place = (lax.axis_index(axis) // stride) % count
    swaps = [
        (axis, [(source, source ^ (step * stride)) for source in range(size)])
        for step in range(1, count)
    ]
    return (count, place, swaps)


def lines():
    n_dp, n_seq = lax.axis_size("dp"), lax.axis_size("seq")
    n_x = 1 << ((n_dp.bit_length() - 1) // 2)
    return {
        "z": line("dp", n_dp, n_dp // n_x, n_x),
        "x": line("dp", n_dp, n_x, 1),
        "y": line("seq", n_seq, n_seq // 2, 2),
        "core": line("seq", n_seq, 2, 1),
    }


def gather_line(block, along):
    count, place, swaps = along
    others = [lax.ppermute(block, axis, swap) for axis, swap in swaps]
    if count == 2:
        first = place == 0
        return jnp.stack([jnp.where(first, block, others[0]), jnp.where(first, others[0], block)])
    whole = jnp.zeros((count,) + block.shape, block.dtype)
    for step, piece in enumerate([block] + others):
        whole = lax.dynamic_update_index_in_dim(whole, piece, place ^ step, 0)
    return whole


def scatter_line(blocks, along, dim, wire):
    count, place, swaps = along
    pick = lambda index: lax.dynamic_index_in_dim(blocks, index, dim, keepdims=False)
    arrived = [
        lax.ppermute(pick(place ^ (step + 1)).astype(wire), axis, swap)
        for step, (axis, swap) in enumerate(swaps)
    ]
    total = pick(place)
    for piece in arrived:
        total = total + piece.astype(F32)
    return total


def gather_rows(shard, ways, split_y):
    n_core, core, _ = ways["core"]
    n_y, y_at, _ = ways["y"]
    rows, columns = shard.shape
    if split_y:
        part = lax.dynamic_slice_in_dim(
            shard, (core * n_y + y_at) * (rows // (2 * n_y)), rows // (2 * n_y), 0
        )
    else:
        part = lax.dynamic_slice_in_dim(shard, core * (rows // 2), rows // 2, 0)
    part = gather_line(part, ways["z"])
    part = gather_line(part, ways["x"])
    if split_y:
        part = gather_line(part, ways["y"])
        part = gather_line(part, ways["core"])
        part = jnp.transpose(part, (3, 2, 0, 1, 4, 5))
    else:
        part = gather_line(part, ways["core"])
        part = jnp.transpose(part, (2, 1, 0, 3, 4))
    return part.reshape(-1, columns)


def scatter_rows(grad, ways, order, wire):
    n_z, n_x, n_y = ways["z"][0], ways["x"][0], ways["y"][0]
    columns = grad.shape[1]
    blocks = grad.reshape(n_z, n_x, 2, n_y, -1, columns)
    blocks = scatter_line(blocks, ways["core"], 2, wire)
    if order == "xy":
        blocks = scatter_line(blocks, ways["x"], 1, wire)
        blocks = scatter_line(blocks, ways["y"], 1, wire)
    else:
        blocks = scatter_line(blocks, ways["y"], 2, wire)
        blocks = scatter_line(blocks, ways["x"], 1, wire)
    return scatter_line(blocks, ways["z"], 0, wire)


def gather_parts(part, ways):
    part = gather_line(part, ways["y"])
    part = gather_line(part, ways["core"])
    return part.reshape(-1, part.shape[-1])


def visible(seg_key, seg_query, pos_query, keys, tile):
    pos_key = lax.broadcasted_iota(jnp.int32, (keys, tile), 0)
    return (seg_key == seg_query) & (pos_key <= pos_query)


def attend_kernel(tile, skip, hd, scale, q_ref, k_ref, v_ref, sq_ref, sk_ref, qp_ref, o_ref, lse_ref):
    length = k_ref.shape[0]
    for head in range(q_ref.shape[1] // hd):
        cols = slice(hd * head, hd * head + hd)
        for step in range(q_ref.shape[0] // tile):
            rows = slice(step * tile, (step + 1) * tile)
            keys = (step + 1) * tile if skip else length
            query = (q_ref[rows, cols].astype(F32) * scale).astype(BF16)
            scores = dot(k_ref[:keys, cols], query, NT)
            allowed = visible(sk_ref[:keys, :], sq_ref[:, rows], qp_ref[:, rows], keys, tile)
            scores = jnp.where(allowed, scores, -1e30)
            top = jnp.max(scores, 0, keepdims=True)
            weight = jnp.exp(scores - top)
            total = jnp.sum(weight, 0, keepdims=True)
            probs = (weight * (1.0 / total)).astype(BF16)
            o_ref[rows, cols] = dot(probs, v_ref[:keys, cols], TN).astype(BF16)
            lse_ref[0, head : head + 1, rows] = top + jnp.log(total)


def attend_back_kernel(
    tile, skip, hd, scale, q_ref, k_ref, v_ref, do_ref, lse_ref, sq_ref, sk_ref, qp_ref,
    dq_ref, dk_ref, dv_ref, dk_sum, dv_sum,
):
    length = k_ref.shape[0]
    dk_sum[...] = jnp.zeros_like(dk_sum)
    dv_sum[...] = jnp.zeros_like(dv_sum)
    for head in range(q_ref.shape[1] // hd):
        cols = slice(hd * head, hd * head + hd)
        for step in range(q_ref.shape[0] // tile):
            rows = slice(step * tile, (step + 1) * tile)
            keys = (step + 1) * tile if skip else length
            query = (q_ref[rows, cols].astype(F32) * scale).astype(BF16)
            key = k_ref[:keys, cols]
            dout = do_ref[rows, cols]
            scores = dot(key, query, NT)
            allowed = visible(sk_ref[:keys, :], sq_ref[:, rows], qp_ref[:, rows], keys, tile)
            scores = jnp.where(allowed, scores, -1e30)
            probs = jnp.exp(scores - lse_ref[0, head : head + 1, rows])
            dprobs = dot(v_ref[:keys, cols], dout, NT)
            delta = jnp.sum(dprobs * probs, 0, keepdims=True)
            dscores = (probs * (dprobs - delta)).astype(BF16)
            dv_sum[:keys, cols] += dot(probs.astype(BF16), dout)
            dk_sum[:keys, cols] += dot(dscores, query)
            dq_ref[rows, cols] = (dot(dscores, key, TN) * scale).astype(dq_ref.dtype)
    dk_ref[...] = dk_sum[...].astype(dk_ref.dtype)
    dv_ref[...] = dv_sum[...].astype(dv_ref.dtype)


def blocks_of(rows, width, offset):
    return pl.BlockSpec((rows, width), lambda pair: (0, pair + offset))


def fixed(shape):
    return pl.BlockSpec(shape, lambda pair: (0, 0))


def kernel_params():
    return pltpu.CompilerParams(vmem_limit_bytes=48 * 2**20)


def attend(qkv, keys, values, offsets, seg_q, seg_k, pos_q, width):
    count, length = qkv.shape[0], keys.shape[0]
    hd = width // HEADS
    lanes = 2 * hd
    pairs = HEADS // 2
    return pl.pallas_call(
        functools.partial(attend_kernel, min(256, count), count == length, hd, hd**-0.5),
        grid=(pairs,),
        in_specs=[
            blocks_of(count, lanes, 0),
            blocks_of(length, lanes, offsets[0]),
            blocks_of(length, lanes, offsets[1]),
            fixed((1, count)),
            fixed((length, 1)),
            fixed((1, count)),
        ],
        out_specs=[blocks_of(count, lanes, 0), pl.BlockSpec((1, 2, count), lambda pair: (pair, 0, 0))],
        out_shape=[
            jax.ShapeDtypeStruct((count, width), BF16),
            jax.ShapeDtypeStruct((pairs, 2, count), F32),
        ],
        cost_estimate=pl.CostEstimate(
            flops=25_000_000_000, bytes_accessed=8_000_000, transcendentals=8_000_000
        ),
        compiler_params=kernel_params(),
    )(qkv, keys, values, seg_q, seg_k, pos_q)


def attend_back(qkv, keys, values, offsets, dout, lse, seg_q, seg_k, pos_q, width, kv_type):
    count, length = qkv.shape[0], keys.shape[0]
    hd = width // HEADS
    lanes = 2 * hd
    pairs = HEADS // 2
    return pl.pallas_call(
        functools.partial(attend_back_kernel, min(256, count), count == length, hd, hd**-0.5),
        grid=(pairs,),
        in_specs=[
            blocks_of(count, lanes, 0),
            blocks_of(length, lanes, offsets[0]),
            blocks_of(length, lanes, offsets[1]),
            blocks_of(count, lanes, 0),
            pl.BlockSpec((1, 2, count), lambda pair: (pair, 0, 0)),
            fixed((1, count)),
            fixed((length, 1)),
            fixed((1, count)),
        ],
        out_specs=[
            blocks_of(count, lanes, 0),
            blocks_of(length, lanes, 0),
            blocks_of(length, lanes, 0),
        ],
        out_shape=[
            jax.ShapeDtypeStruct((count, width), BF16),
            jax.ShapeDtypeStruct((length, width), kv_type),
            jax.ShapeDtypeStruct((length, width), kv_type),
        ],
        scratch_shapes=[pltpu.VMEM((length, lanes), F32)] * 2,
        cost_estimate=pl.CostEstimate(
            flops=40_000_000_000, bytes_accessed=12_000_000, transcendentals=8_000_000
        ),
        compiler_params=kernel_params(),
    )(qkv, keys, values, dout, lse, seg_q, seg_k, pos_q)


def layer_norm(hidden, gain, shift):
    mean = jnp.mean(hidden, -1, keepdims=True)
    centred = hidden - mean
    var = jnp.mean(centred * centred, -1, keepdims=True)
    rstd = lax.rsqrt(var + NORM_EPS)
    unit = centred * rstd
    return (unit * gain + shift, unit, rstd)


def norm_back(grad, unit, rstd, gain):
    dunit = grad * gain
    dhid = rstd * (
        dunit
        - jnp.mean(dunit, -1, keepdims=True)
        - unit * jnp.mean(dunit * unit, -1, keepdims=True)
    )
    return (dhid, jnp.sum(grad * unit, 0), jnp.sum(grad, 0))


def adamw(weight, first, second, grad, rate, decay):
    new_first = BETA_ONE * first + (1.0 - BETA_ONE) * grad
    new_second = BETA_TWO * second + (1.0 - BETA_TWO) * grad * grad
    first_hat = new_first / (1.0 - BETA_ONE**STEP)
    second_hat = new_second / (1.0 - BETA_TWO**STEP)
    return (
        weight - rate * (first_hat / (jnp.sqrt(second_hat) + ADAM_EPS) + decay * weight),
        new_first,
        new_second,
    )


def body(*args):
    patches, segments = args[:2]
    masters, firsts, seconds = (args[2:10], args[10:18], args[18:26])
    embed_in, pos_table, attn_qkv, attn_out, mlp_up, mlp_down, head_out, vectors = masters
    ways = lines()
    n_seq = lax.axis_size("seq")
    seq_at = lax.axis_index("seq")
    micros, group = segments.shape[0], segments.shape[2]
    length = group * n_seq
    width = attn_qkv.shape[1] // 3

    share = max(1, n_seq // micros)
    count = length // share
    mine = seq_at // share
    patches = patches.reshape(micros, PATCH, group)
    segments = segments.reshape(micros, group)
    if share == 1:
        swaps = [
            ("seq", [(source, source ^ step) for source in range(n_seq)]) for step in range(1, n_seq)
        ]
        row = jnp.zeros((n_seq, PATCH, group), BF16)
        seg = jnp.zeros((n_seq, group), jnp.int32)
        for step in range(n_seq):
            piece = lax.dynamic_index_in_dim(patches, seq_at ^ step, 0, keepdims=False)
            ids = lax.dynamic_index_in_dim(segments, seq_at ^ step, 0, keepdims=False)
            if step:
                piece = lax.ppermute(piece, *swaps[step - 1])
                ids = lax.ppermute(ids, *swaps[step - 1])
            row = lax.dynamic_update_index_in_dim(row, piece, seq_at ^ step, 0)
            seg = lax.dynamic_update_index_in_dim(seg, ids, seq_at ^ step, 0)
        row = jnp.swapaxes(row, 0, 1).reshape(PATCH, length)
        seg = seg.reshape(length)
    else:
        row = lax.all_gather(patches, "seq", axis=2, tiled=True)
        seg = lax.all_gather(segments, "seq", axis=1, tiled=True)
        row = lax.dynamic_index_in_dim(row, mine, 0, keepdims=False)
        seg = lax.dynamic_index_in_dim(seg, mine, 0, keepdims=False)
    start = (seq_at % share) * count
    part = lambda value: lax.dynamic_slice_in_dim(value, start, count, 0)

    low = lambda value: value.astype(BF16)
    early = jnp.concatenate(
        [low(attn_qkv), low(pos_table).T, low(embed_in).T, low(vectors).T], axis=1
    )
    early = gather_rows(early, ways, False)
    w_qkv = early[:, : 3 * width]
    w_pos = early[:, 3 * width : 3 * width + length + PATCH]
    gains = early[:, 3 * width + length + PATCH :].astype(F32).T
    w_attn = gather_rows(jnp.concatenate([low(attn_out), low(head_out)], axis=1), ways, False)
    w_head = w_attn[:, width:]
    w_attn = w_attn[:, :width]
    w_up = gather_rows(low(mlp_up), ways, True)
    w_down = gather_rows(low(mlp_down).T, ways, True)

    at = jnp.arange(length)
    begins = jnp.zeros((length,), jnp.int32)
    for image in range(5):
        before = (seg > 0) & (seg < image) if image else seg > 0
        begins = jnp.where(seg == image, jnp.sum(before.astype(jnp.int32)), begins)
    offset = part(at - begins)
    own = part(seg)
    tokens = part(row.T)
    later = part(jnp.concatenate([row[:, 1:], jnp.zeros((PATCH, 1), BF16)], axis=1).T)
    seg_next = part(jnp.concatenate([seg[1:], jnp.zeros((1,), jnp.int32)]))
    pair = ((own == seg_next) & (own > 0)).astype(F32)[:, None]
    first = ((own > 0) & (offset == 0)).astype(F32)[:, None]
    valid = jnp.sum((own > 0).astype(jnp.int32)).astype(F32) * PATCH
    lookup = (offset[:, None] == jnp.arange(length)[None, :]).astype(BF16)
    inputs = jnp.concatenate([lookup, tokens], axis=1)
    seg_q, seg_k, pos_q = (own[None, :], seg[:, None], part(at)[None, :].astype(jnp.int32))

    h0 = dot(inputs, w_pos, NT) + (gains[6] - 1.0)
    normed, unit_one, rstd_one = layer_norm(h0, gains[0], gains[1] - 1.0)
    normed = low(normed)
    qkv = low(dot(normed, w_qkv))
    if share == 1:
        keys, values, offsets = (qkv, qkv, (HEADS // 2, HEADS))
    else:
        near = [list(range(g, g + share)) for g in range(0, n_seq, share)]
        keys = lax.all_gather(qkv[:, width:], "seq", axis=0, tiled=True, axis_index_groups=near)
        values, offsets = (keys, (0, HEADS // 2))
    attended, lse = attend(qkv, keys, values, offsets, seg_q, seg_k, pos_q, width)
    h1 = h0 + dot(attended, w_attn) + (gains[7] - 1.0)
    mixed, unit_two, rstd_two = layer_norm(h1, gains[2], gains[3] - 1.0)
    mixed = low(mixed)
    upper = dot(mixed, w_up)
    hidden = low(jax.nn.gelu(upper))
    h2 = h1 + dot(hidden, w_down, NT)
    final, unit_fin, rstd_fin = layer_norm(h2, gains[4], gains[5] - 1.0)
    final = low(final)
    out = dot(final, w_head)
    alpha = out[:, PATCH:]
    shrink = jnp.exp(-alpha)
    scaled = (later.astype(F32) - out[:, :PATCH]) * shrink
    plain = tokens.astype(F32)
    total = jnp.sum(pair * (0.5 * scaled * scaled + alpha)) + jnp.sum(first * 0.5 * plain * plain)

    dout = low(jnp.concatenate([-pair * scaled * shrink, pair * (1.0 - scaled * scaled)], axis=1))
    grad_head = dot(final, dout, TN)
    dh2, gain_fin, shift_fin = norm_back(dot(dout, w_head, NT), unit_fin, rstd_fin, gains[4])
    ddown = low(dh2)
    grad_down = dot(ddown, hidden, TN)
    _, gelu_back = jax.vjp(jax.nn.gelu, upper)
    dupper = low(gelu_back(dot(ddown, w_down))[0])
    grad_up = dot(mixed, dupper, TN)
    dnorm, gain_two, shift_two = norm_back(dot(dupper, w_up, NT), unit_two, rstd_two, gains[2])
    dh1 = dh2 + dnorm
    dattn = low(dh1)
    grad_attn = dot(attended, dattn, TN)
    dattended = low(dot(dattn, w_attn, NT))
    dquery, dkeys, dvalues = attend_back(
        qkv, keys, values, offsets, dattended, lse, seg_q, seg_k, pos_q, width,
        BF16 if share == 1 else F32,
    )
    if share > 1:
        dkeys, dvalues = (
            low(lax.psum_scatter(d, "seq", scatter_dimension=0, tiled=True, axis_index_groups=near))
            for d in (dkeys, dvalues)
        )
    dqkv = jnp.concatenate([dquery, dkeys, dvalues], axis=1)
    grad_qkv = dot(normed, dqkv, TN)
    dnorm, gain_one, shift_one = norm_back(dot(dqkv, w_qkv, NT), unit_one, rstd_one, gains[0])
    dh0 = dh1 + dnorm
    high = low(dh0)
    rest = low(dh0 - high.astype(F32))
    grad_pos = dot(high, inputs, TN)
    grad_pos = jnp.concatenate(
        [grad_pos[:, :length] + dot(rest, lookup, TN), grad_pos[:, length:]], axis=1
    )
    grad_vec = jnp.stack(
        [
            gain_one,
            shift_one,
            gain_two,
            shift_two,
            gain_fin,
            shift_fin,
            jnp.sum(dh0, 0),
            jnp.sum(dh1, 0),
        ],
        axis=1,
    )

    parts = [
        scatter_rows(grad_down, ways, "xy", WIRE),
        scatter_rows(grad_up, ways, "yx", WIRE),
        scatter_rows(grad_attn, ways, "xy", WIRE),
        scatter_rows(grad_qkv, ways, "yx", WIRE),
        scatter_rows(grad_pos[:, :length], ways, "xy", WIRE),
        scatter_rows(
            jnp.concatenate([grad_head, grad_pos[:, length:], grad_vec], axis=1), ways, "xy", F32
        ),
    ]
    squares = sum(jnp.sum(p * p) for p in parts)
    squares, total, valid = lax.psum((squares, total, valid), ("dp", "seq"))
    down, up, attn, wide, table, small = [gather_parts(p, ways) for p in parts]
    outs = head_out.shape[1]
    pieces = [
        small[:, outs : outs + PATCH].T,
        table.T,
        wide,
        attn,
        up,
        down.T,
        small[:, :outs],
        small[:, outs + PATCH :].T,
    ]
    norm = jnp.sqrt(squares) / valid
    clip = jnp.minimum(1.0, CLIP_AT / (norm + 1e-06))
    results = [
        adamw(
            masters[i],
            firsts[i],
            seconds[i],
            pieces[i] / valid * clip,
            RATE if i < 7 else VEC_RATE,
            DECAY if i < 7 else 0.0,
        )
        for i in range(8)
    ]
    return (
        total / math.log(2.0),
        valid,
        norm,
        *[r[0] for r in results],
        *[r[1] for r in results],
        *[r[2] for r in results],
    )


def solution(mesh):
    rows, columns = (P("dp", None), P(None, "dp"))
    weights = (columns, columns, rows, rows, rows, columns, rows, columns)
    in_specs = (P(None, "dp", None, "seq"), P(None, "dp", "seq")) + weights * 3
    out_specs = (P(), P(), P()) + weights * 3
    return jax.shard_map(body, mesh=mesh, in_specs=in_specs, out_specs=out_specs, check_vma=False)
```

time: 2090 us -> 653 us (0.31)
  waiting for transfers between devices: 1280 us -> 174 us
  matrix products: 357 us -> 96.2 us
  blocking collectives: 135 us -> 40.1 us
  starting transfers between devices: 2.5 us -> 82.9 us
  Pallas kernels: 0 us -> 60.8 us
  other arithmetic: 146 us -> 93.8 us
  local copies, waits for them, and re-layouts: 127 us -> 78.8 us
    reduce_scatter x14 -> x0, waiting for transfers between devices: 759 us -> none  [the longest x1 167 us: body(): lax.psum_scatter(grads[4], 'dp', scatter_dimension=0, tiled=True)]
    all_gather x13 -> x0, waiting for transfers between devices: 323 us -> none  [the longest x1 81 us: body(): lax.all_gather(mlp_up.astype(jnp.bfloat16), 'dp', axis=0, tiled=True)]
    dot_general x92 -> x18, matrix products: 357 us -> 96.2 us  [dot(): return lax.dot_general(left, right, dims, preferred_element_type=F32)]
    ppermute x1 -> x76, waiting for transfers between devices: 0.01 us -> 174 us  [the longest x34 95.3 us: gather_line(): others = [lax.ppermute(block, axis, swap) for axis, swap in swaps]]
    unnamed x16 -> x0, waiting for transfers between devices: 128 us -> none
    all_gather x4 -> x0, blocking collectives: 99.7 us -> none  [the longest x1 33.7 us: body(): lax.all_gather(head_out.astype(jnp.bfloat16), 'dp', axis=0, tiled=True)]
    ppermute x1 -> x76, starting transfers between devices: 1.28 us -> 82.9 us  [the longest x34 39.7 us: gather_line(): others = [lax.ppermute(block, axis, swap) for axis, swap in swaps]]
    psum x1 -> x0, waiting for transfers between devices: 69 us -> none  [body(): lax.psum((shards[0], shards[1], shards[2], shards[3], shards[4], shards[5...]
  transfers between devices with their start and end apart: 31 -> 76, of which waited for: 25 -> 33; matrix products, arithmetic and copies ran while one was open for 14% -> 20% of each run, Pallas kernels for 0% -> 3%
where the time goes in v1:
time: 653 us; the launch traced here: 641 us
  waiting for transfers between devices  174 us (27%)
  matrix products  96.2 us (15%)
  other arithmetic  93.8 us (14%)
  starting transfers between devices  82.9 us (13%)
  local copies, waits for them, and re-layouts  78.8 us (12%)
  Pallas kernels  60.8 us (9%)
  blocking collectives  40.1 us (6%)
  between operations  13.8 us (2%)
    dot_general x18, matrix products, dot(): return lax.dot_general(left, right, dims, preferred_element_type=F32)  96.2 us
    ppermute x34, waiting for transfers between devices, gather_line(): others = [lax.ppermute(block, axis, swap) for axis, swap in swaps]  95.3 us
    ppermute x36, waiting for transfers between devices, scatter_line(): lax.ppermute(pick(place ^ step + 1).astype(wire), axis, swap)  79.1 us
    psum x1, blocking collectives, body(): squares, total, valid = lax.psum((squares, total, valid), ('dp', 'seq'))  40.1 us
    ppermute x34, starting transfers between devices, gather_line(): others = [lax.ppermute(block, axis, swap) for axis, swap in swaps]  39.7 us
    ppermute x36, starting transfers between devices, scatter_line(): lax.ppermute(pick(place ^ step + 1).astype(wire), axis, swap)  39.4 us
    pallas_call x1, Pallas kernels, attend_back(): pl.pallas_call(functools.partial(attend_back_kernel, min(256, count), cou...  38.3 us
    pallas_call x1, Pallas kernels, attend(): pl.pallas_call(functools.partial(attend_kernel, min(256, count), count ==...  22.4 us
  transfers between devices with their start and end apart: 76, of which 33 were waited for; matrix products, arithmetic and copies ran while one was open for 20% of the time, Pallas kernels for 3%

profile of v1, /device:TPU:0, one launch (start us, length us, event | category | flops | bytes accessed | tf_op | source)
XLA Modules:
  0.0 641.0 jit_solution(10859726078236575465)
XLA Ops:
  3.2 3.0 collective-permute-start.11
  6.3 2.6 collective-permute-start.12
  29.0 3.2 select_subtract_fusion
  34.0 3.9 fusion.140
  42.2 3.4 collective-permute-start.7
  57.7 3.9 collective-permute-start.17
  62.5 7.7 %collective-permute-done.16 = bf16[24,3072]{1,0:T(8,128)(2,1)S(1)} collective-permute-done((bf16[24,3072]{1,0:T(8,128)(2,1)}, bf16[24,3072]{1,0:T(8,128)(2,1)S(1)}, u32[]{:S(2)}, u32[]{:S(2)}) %collective-permute-start.16) | collective-permute-done | bytes 147488 | tf_op jit(solution)/shard_map/ppermute | solution.py:57
  70.2 3.3 collective-permute-start.18
  73.5 11.6 %collective-permute-done.17 = bf16[24,3072]{1,0:T(8,128)(2,1)S(1)} collective-permute-done((bf16[24,3072]{1,0:T(8,128)(2,1)}, bf16[24,3072]{1,0:T(8,128)(2,1)S(1)}, u32[]{:S(2)}, u32[]{:S(2)}) %collective-permute-start.17) | collective-permute-done | bytes 147488 | tf_op jit(solution)/shard_map/ppermute | solution.py:57
  85.2 4.1 collective-permute-start.23
  89.3 2.5 collective-permute-done.22
  91.8 3.2 collective-permute-start.24
  95.0 5.6 collective-permute-done.23
  106.9 4.6 collective-permute-done.14
  111.8 12.4 %collective-permute-done.19 = bf16[4,24,3072]{2,1,0:T(8,128)(2,1)S(1)} collective-permute-done((bf16[4,24,3072]{2,1,0:T(8,128)(2,1)S(1)}, bf16[4,24,3072]{2,1,0:T(8,128)(2,1)S(1)}, u32[]{:S(2)}, u32[]{:S(2)}) %collective-permute-start.19) | collective-permute-done | bytes 589856 | tf_op jit(solution)/shard_map/ppermute | solution.py:57
  126.0 10.8 %collective-permute-done.25 = bf16[4,24,3072]{2,1,0:T(8,128)(2,1)S(1)} collective-permute-done((bf16[4,24,3072]{2,1,0:T(8,128)(2,1)S(1)}, bf16[4,24,3072]{2,1,0:T(8,128)(2,1)S(1)}, u32[]{:S(2)}, u32[]{:S(2)}) %collective-permute-start.25) | collective-permute-done | bytes 589856 | tf_op jit(solution)/shard_map/ppermute | solution.py:57
  138.6 21.7 %collective-permute-done.9 = bf16[4,48,3384]{2,1,0:T(8,128)(2,1)S(1)} collective-permute-done((bf16[4,48,3384]{2,1,0:T(8,128)(2,1)S(1)}, bf16[4,48,3384]{2,1,0:T(8,128)(2,1)S(1)}, u32[]{:S(2)}, u32[]{:S(2)}) %collective-permute-start.9) | collective-permute-done | bytes 1299488 | tf_op jit(solution)/shard_map/ppermute | solution.py:57
  163.4 4.5 collective-permute-done.26
  177.0 7.2 %convolution_convert_fusion.q_ref.k_ref.v_ref = bf16[1024,2304]{1,0:T(8,128)(2,1)} fusion(bf16[768,3384]{1,0:T(8,128)(2,1)S(1)} %bitcast.440, f32[768]{0:T(1024)S(1)} %get-tuple-element.132, f32[768]{0:T(1024)S(1)} %get-tuple-element.133, f32[1024]{0:T(1024)S(1)} %add_rsqrt_fusion.2, f32[1024]{0:T(1024)S(1)} %broadcast_multiply_fusion.8, ...), kind=kOutput, calls=%fused_computation.10 | convolution fusion | flops 3630956544 | bytes 11423744 | tf_op jit(solution)/shard_map/dot_general | solution.py:32
  184.2 22.4 %shard_map.457 = (bf16[1024,768]{1,0:T(8,128)(2,1)S(1)}, f32[6,2,1024]{2,1,0:T(2,128)S(1)}) custom-call(bf16[1024,2304]{1,0:T(8,128)(2,1)} %convolution_convert_fusion.q_ref.k_ref.v_ref, bf16[1024,2304]{1,0:T(8,128)(2,1)} %convolution_convert_fusion.q_ref.k_ref.v_ref, bf16[1024,2304]{1,0:T(8,128)(2,1)} %convolution_convert_fusion.q_ref.k_ref.v_ref, ...), custom_call_target="tpu_custom_call" | custom-call | flops 24999999488 | bytes 8000000 | tf_op jit(solution)/shard_map/pallas_call | solution.py:192
  208.9 2.7 select_bitcast_fusion.3
  212.0 2.6 copy.213
  217.1 5.3 fusion.114
  222.4 11.3 %fusion.144 = (f32[1024]{0:T(1024)S(1)}, f32[1024,768]{0,1:T(8,128)S(1)}) fusion(f32[1024,768]{0,1:T(8,128)S(1)} %get-tuple-element.269, bf16[768,3072]{1,0:T(8,128)(2,1)} %bitcast.452, f32[1024,3072]{1,0:T(8,128)S(1)} %fusion.114), kind=kOutput, calls=%fused_computation.387 | convolution fusion | flops 4861721600 | bytes 23597056 | tf_op jit(solution)/shard_map/dot_general | solution.py:32
  240.9 3.6 copy.215
  244.6 4.0 multiply_reduce_fusion
  250.1 18.4 %fusion.6 = bf16[1024,3072]{1,0:T(8,128)(2,1)S(1)} fusion(f32[1024,3072]{1,0:T(8,128)} %copy-done.13, bf16[768,3072]{1,0:T(8,128)(2,1)} %bitcast.453, f32[1024,768]{0,1:T(8,128)S(1)} %subtract_multiply_fusion), kind=kOutput, calls=%fused_computation.8 | convolution fusion | flops 4895539200 | bytes 26738688 | tf_op jit(solution)/shard_map/dot_general | solution.py:32
  268.5 6.7 %fusion.146 = (f32[768]{0:T(1024)S(1)}, f32[1024,768]{1,0:T(8,128)}) fusion(bf16[1024,3072]{1,0:T(8,128)(2,1)S(1)} %fusion.6, bf16[768,3072]{1,0:T(8,128)(2,1)S(1)} %bitcast.433), kind=kOutput, calls=%fused_computation.389 | convolution fusion | flops 4832623616 | bytes 14158848 | tf_op jit(solution)/shard_map/dot_general | solution.py:32
  275.2 3.6 copy.218
  278.8 4.0 multiply_reduce_fusion.1
  283.5 3.2 fusion.132
  286.8 2.6 convolution_convert_fusion.1.do_ref
  289.4 38.3 %shard_map.458 = (bf16[1024,768]{1,0:T(8,128)(2,1)S(1)}, bf16[1024,768]{1,0:T(8,128)(2,1)S(1)}, bf16[1024,768]{1,0:T(8,128)(2,1)S(1)}) custom-call(bf16[1024,2304]{1,0:T(8,128)(2,1)} %convolution_convert_fusion.q_ref.k_ref.v_ref, bf16[1024,2304]{1,0:T(8,128)(2,1)} %convolution_convert_fusion.q_ref.k_ref.v_ref, ...), custom_call_target="tpu_custom_call" | custom-call | flops 40000000000 | bytes 12000000 | tf_op jit(solution)/shard_map/pallas_call | solution.py:220
  328.1 5.6 fusion.145
  333.7 3.9 copy.220
  337.7 3.2 multiply_reduce_fusion.2
  345.2 4.0 slice_add_fusion
  349.3 6.4 fusion.115
  355.7 7.9 %fusion.113 = f32[768,3072]{1,0:T(8,128)} fusion(bf16[1024,3072]{1,0:T(8,128)(2,1)S(1)} %bitcast.483, f32[1024,768]{0,1:T(8,128)S(1)} %copy-done.4, f32[768]{0:T(1024)S(1)} %get-tuple-element.129, f32[768]{0:T(1024)S(1)} %get-tuple-element.130, f32[1024]{0:T(1024)S(1)} %add_rsqrt_fusion.1, f32[1024]{0:T(1024)S(1)} %broadcast_multiply_fusion.7), kind=kOutput, calls=%fused_computation.380 | convolution fusion | flops 4835770368 | bytes 18888704 | tf_op jit(solution)/shard_map/dot_general | solution.py:32
  363.6 7.5 %fusion.40 = f32[768,3072]{1,0:T(8,128)} fusion(f32[1024,768]{0,1:T(8,128)S(1)} %copy-done.17, f32[1024,3072]{1,0:T(8,128)S(1)} %bitcast.435), kind=kOutput, calls=%fused_computation.130 | convolution fusion | flops 4860936192 | bytes 25165824 | tf_op jit(solution)/shard_map/dot_general | solution.py:32
  374.9 3.0 concatenate.70
  378.5 3.8 copy.222
  382.3 2.4 fusion.33
  384.9 3.3 fusion.37
  389.9 3.4 fusion.15
  397.2 4.1 fusion.13
  411.2 4.1 fusion.12
  421.7 6.5 %collective-permute-done.41 = bf16[4,2,24,768]{3,2,1,0:T(8,128)(2,1)S(1)} collective-permute-done((bf16[4,2,24,768]{3,2,1,0:T(8,128)(2,1)S(1)}, bf16[4,2,24,768]{3,2,1,0:T(8,128)(2,1)S(1)}, u32[]{:S(2)}, u32[]{:S(2)}) %collective-permute-start.41) | collective-permute-done | bytes 294944 | tf_op jit(solution)/shard_map/ppermute | solution.py:71
  437.7 4.2 collective-permute-done.53
  451.3 2.5 collective-permute-start.56
  456.3 3.3 collective-permute-done.57
  460.8 3.2 bitcast_add_fusion.2
  467.6 15.4 %collective-permute-done.47 = bf16[4,2,24,2304]{3,2,1,0:T(8,128)(2,1)S(1)} collective-permute-done((bf16[4,2,24,2304]{3,2,1,0:T(8,128)(2,1)S(1)}, bf16[4,2,24,2304]{3,2,1,0:T(8,128)(2,1)S(1)}, u32[]{:S(2)}, u32[]{:S(2)}) %collective-permute-start.47) | collective-permute-done | bytes 884768 | tf_op jit(solution)/shard_map/ppermute | solution.py:71
  484.9 3.4 bitcast_add_fusion
  496.4 2.6 bitcast_add_fusion.1
  505.0 12.1 %collective-permute-done.68 = f32[24,2304]{1,0:T(8,128)S(1)} collective-permute-done((f32[24,2304]{1,0:T(8,128)S(1)}, f32[24,2304]{1,0:T(8,128)S(1)}, u32[]{:S(2)}, u32[]{:S(2)}) %collective-permute-start.68) | collective-permute-done | bytes 221216 | tf_op jit(solution)/shard_map/ppermute | solution.py:57
  518.5 10.0 %collective-permute-done.29 = bf16[4,2,24,3072]{3,2,1,0:T(8,128)(2,1)S(1)} collective-permute-done((bf16[4,2,24,3072]{3,2,1,0:T(8,128)(2,1)S(1)}, bf16[4,2,24,3072]{3,2,1,0:T(8,128)(2,1)S(1)}, u32[]{:S(2)}, u32[]{:S(2)}) %collective-permute-start.29) | collective-permute-done | bytes 1179680 | tf_op jit(solution)/shard_map/ppermute | solution.py:71
  529.2 8.4 %collective-permute-done.36 = bf16[4,24,3072]{2,1,0:T(8,128)(2,1)S(1)} collective-permute-done((bf16[4,24,3072]{2,1,0:T(8,128)(2,1)S(1)}, bf16[4,24,3072]{2,1,0:T(8,128)(2,1)S(1)}, u32[]{:S(2)}, u32[]{:S(2)}) %collective-permute-start.36) | collective-permute-done | bytes 589856 | tf_op jit(solution)/shard_map/ppermute | solution.py:71
  543.3 4.0 collective-permute-done.37
  547.3 6.2 collective-permute-done.38
  556.2 5.8 collective-permute-done.32
  567.8 40.1 %all-reduce.1 = (f32[]{:T(128)}, f32[]{:T(128)}, f32[]{:T(128)}) all-reduce(f32[]{:T(128)S(6)} %add.590, f32[]{:T(128)S(6)} %mul.660, f32[]{:T(128)S(6)} %add.640), channel_id=1, replica_groups=mesh['dp'=8,'seq'=4] {'dp','seq'}, use_global_device_ids=true, to_apply=%region_13.14 | all-reduce | flops 3 | bytes 24 | tf_op jit(solution)/shard_map/psum | solution.py:436
  608.6 2.5 collective-permute-start.74
  620.0 3.5 multiply_subtract_fusion.2
  (494 shorter events, 182.7 us)
Async XLA Ops:
  3.2 52.0 %collective-permute-start.11 = (bf16[48,864]{1,0:T(8,128)(2,1)}, bf16[48,864]{1,0:T(8,128)(2,1)}, u32[]{:S(2)}, u32[]{:S(2)}) collective-permute-start(bf16[48,864]{1,0:T(8,128)(2,1)} %get-tuple-element.190), channel_id=1, source_target_pairs={{0,8},{4,12},{8,0},{12,4},{16,24},{20,28},{24,16},{28,20},{1,9},{5... | collective-permute-start | bytes 248840 | tf_op jit(solution)/shard_map/ppermute | solution.py:57
  6.3 50.4 %collective-permute-start.12 = (bf16[48,864]{1,0:T(8,128)(2,1)}, bf16[48,864]{1,0:T(8,128)(2,1)}, u32[]{:S(2)}, u32[]{:S(2)}) collective-permute-start(bf16[48,864]{1,0:T(8,128)(2,1)} %get-tuple-element.190), channel_id=1, source_target_pairs={{0,16},{4,20},{8,24},{12,28},{16,0},{20,4},{24,8},{28,12},{1,17},{... | collective-permute-start | bytes 248840 | tf_op jit(solution)/shard_map/ppermute | solution.py:57
  10.1 13.6 %collective-permute-start = (s32[256]{0:T(256)S(1)}, s32[256]{0:T(256)S(1)}, u32[]{:S(2)}, u32[]{:S(2)}) collective-permute-start(s32[256]{0:T(256)S(1)} %bitcast.481), channel_id=1, source_target_pairs={{0,1},{1,0},{2,3},{3,2},{4,5},{5,4},{6,7},{7,6},{8,9},{9,8},{10,11... | collective-permute-start | bytes 3080 | tf_op jit(solution)/shard_map/ppermute | solution.py:309
  10.1 15.1 %collective-permute-start.1 = (s32[256]{0:T(256)}, s32[256]{0:T(256)}, u32[]{:S(2)}, u32[]{:S(2)}) collective-permute-start(s32[256]{0:T(256)} %bitcast.3), channel_id=1, source_target_pairs={{0,2},{1,3},{2,0},{3,1},{4,6},{5,7},{6,4},{7,5},{8,10},{9,11},{10,... | collective-permute-start | bytes 3080 | tf_op jit(solution)/shard_map/ppermute | solution.py:309
  11.7 15.8 %collective-permute-start.2 = (s32[256]{0:T(256)S(1)}, s32[256]{0:T(256)}, u32[]{:S(2)}, u32[]{:S(2)}) collective-permute-start(s32[256]{0:T(256)S(1)} %bitcast.479), channel_id=1, source_target_pairs={{0,3},{1,2},{2,1},{3,0},{4,7},{5,6},{6,5},{7,4},{8,11},{9,10},{10,... | collective-permute-start | bytes 3080 | tf_op jit(solution)/shard_map/ppermute | solution.py:309
  24.3 14.6 %collective-permute-start.3 = (bf16[48,256]{1,0:T(8,128)(2,1)S(1)}, bf16[48,256]{1,0:T(8,128)(2,1)S(1)}, u32[]{:S(2)}, u32[]{:S(2)}) collective-permute-start(bf16[48,256]{1,0:T(8,128)(2,1)S(1)} %get-tuple-element.256), channel_id=1, source_target_pairs={{0,1},{1,0},{2,3},{3,2},{4,5},{5,4},{6,7},{7,6},{8,9},{9,8},{10,11... | collective-permute-start | bytes 73736 | tf_op jit(solution)/shard_map/ppermute | solution.py:308
  25.3 15.0 %collective-permute-start.4 = (bf16[48,256]{1,0:T(8,128)(2,1)}, bf16[48,256]{1,0:T(8,128)(2,1)}, u32[]{:S(2)}, u32[]{:S(2)}) collective-permute-start(bf16[48,256]{1,0:T(8,128)(2,1)} %get-tuple-element.258), channel_id=1, source_target_pairs={{0,2},{1,3},{2,0},{3,1},{4,6},{5,7},{6,4},{7,5},{8,10},{9,11},{10,... | collective-permute-start | bytes 73736 | tf_op jit(solution)/shard_map/ppermute | solution.py:308
  27.5 14.7 %collective-permute-start.5 = (bf16[48,256]{1,0:T(8,128)(2,1)S(1)}, bf16[48,256]{1,0:T(8,128)(2,1)}, u32[]{:S(2)}, u32[]{:S(2)}) collective-permute-start(bf16[48,256]{1,0:T(8,128)(2,1)S(1)} %get-tuple-element.255), channel_id=1, source_target_pairs={{0,3},{1,2},{2,1},{3,0},{4,7},{5,6},{6,5},{7,4},{8,11},{9,10},{10,... | collective-permute-start | bytes 73736 | tf_op jit(solution)/shard_map/ppermute | solution.py:308
  38.9 18.9 %collective-permute-start.13 = (bf16[48,864]{1,0:T(8,128)(2,1)}, bf16[48,864]{1,0:T(8,128)(2,1)}, u32[]{:S(2)}, u32[]{:S(2)}) collective-permute-start(bf16[48,864]{1,0:T(8,128)(2,1)} %get-tuple-element.190), channel_id=1, source_target_pairs={{0,24},{4,28},{8,16},{12,20},{16,8},{20,12},{24,0},{28,4},{1,25},{... | collective-permute-start | bytes 248840 | tf_op jit(solution)/shard_map/ppermute | solution.py:57
  40.2 62.4 %collective-permute-start.6 = (bf16[48,3384]{1,0:T(8,128)(2,1)}, bf16[48,3384]{1,0:T(8,128)(2,1)}, u32[]{:S(2)}, u32[]{:S(2)}) collective-permute-start(bf16[48,3384]{1,0:T(8,128)(2,1)} %get-tuple-element.192), channel_id=1, source_target_pairs={{0,8},{4,12},{8,0},{12,4},{16,24},{20,28},{24,16},{28,20},{1,9},{5... | collective-permute-start | bytes 974600 | tf_op jit(solution)/shard_map/ppermute | solution.py:57
  42.2 63.1 %collective-permute-start.7 = (bf16[48,3384]{1,0:T(8,128)(2,1)}, bf16[48,3384]{1,0:T(8,128)(2,1)}, u32[]{:S(2)}, u32[]{:S(2)}) collective-permute-start(bf16[48,3384]{1,0:T(8,128)(2,1)} %get-tuple-element.192), channel_id=1, source_target_pairs={{0,16},{4,20},{8,24},{12,28},{16,0},{20,4},{24,8},{28,12},{1,17},{... | collective-permute-start | bytes 974600 | tf_op jit(solution)/shard_map/ppermute | solution.py:57
  55.2 51.0 %collective-permute-start.8 = (bf16[48,3384]{1,0:T(8,128)(2,1)}, bf16[48,3384]{1,0:T(8,128)(2,1)S(1)}, u32[]{:S(2)}, u32[]{:S(2)}) collective-permute-start(bf16[48,3384]{1,0:T(8,128)(2,1)} %get-tuple-element.192), channel_id=1, source_target_pairs={{0,24},{4,28},{8,16},{12,20},{16,8},{20,12},{24,0},{28,4},{1,25},{... | collective-permute-start | bytes 974600 | tf_op jit(solution)/shard_map/ppermute | solution.py:57
  56.7 13.5 %collective-permute-start.16 = (bf16[24,3072]{1,0:T(8,128)(2,1)}, bf16[24,3072]{1,0:T(8,128)(2,1)S(1)}, u32[]{:S(2)}, u32[]{:S(2)}) collective-permute-start(bf16[24,3072]{1,0:T(8,128)(2,1)} %get-tuple-element.188), channel_id=1, source_target_pairs={{0,8},{4,12},{8,0},{12,4},{16,24},{20,28},{24,16},{28,20},{1,9},{5... | collective-permute-start | bytes 442376 | tf_op jit(solution)/shard_map/ppermute | solution.py:57
  57.7 27.4 %collective-permute-start.17 = (bf16[24,3072]{1,0:T(8,128)(2,1)}, bf16[24,3072]{1,0:T(8,128)(2,1)S(1)}, u32[]{:S(2)}, u32[]{:S(2)}) collective-permute-start(bf16[24,3072]{1,0:T(8,128)(2,1)} %get-tuple-element.188), channel_id=1, source_target_pairs={{0,16},{4,20},{8,24},{12,28},{16,0},{20,4},{24,8},{28,12},{1,17},{... | collective-permute-start | bytes 442376 | tf_op jit(solution)/shard_map/ppermute | solution.py:57
  70.2 15.0 %collective-permute-start.18 = (bf16[24,3072]{1,0:T(8,128)(2,1)}, bf16[24,3072]{1,0:T(8,128)(2,1)S(1)}, u32[]{:S(2)}, u32[]{:S(2)}) collective-permute-start(bf16[24,3072]{1,0:T(8,128)(2,1)} %get-tuple-element.188), channel_id=1, source_target_pairs={{0,24},{4,28},{8,16},{12,20},{16,8},{20,12},{24,0},{28,4},{1,25},{... | collective-permute-start | bytes 442376 | tf_op jit(solution)/shard_map/ppermute | solution.py:57
  85.1 6.6 %collective-permute-start.22 = (bf16[24,3072]{1,0:T(8,128)(2,1)}, bf16[24,3072]{1,0:T(8,128)(2,1)S(1)}, u32[]{:S(2)}, u32[]{:S(2)}) collective-permute-start(bf16[24,3072]{1,0:T(8,128)(2,1)} %fusion.91), channel_id=1, source_target_pairs={{0,8},{4,12},{8,0},{12,4},{16,24},{20,28},{24,16},{28,20},{1,9},{5... | collective-permute-start | bytes 442376 | tf_op jit(solution)/shard_map/ppermute | solution.py:57
  85.2 15.4 %collective-permute-start.23 = (bf16[24,3072]{1,0:T(8,128)(2,1)}, bf16[24,3072]{1,0:T(8,128)(2,1)S(1)}, u32[]{:S(2)}, u32[]{:S(2)}) collective-permute-start(bf16[24,3072]{1,0:T(8,128)(2,1)} %fusion.91), channel_id=1, source_target_pairs={{0,16},{4,20},{8,24},{12,28},{16,0},{20,4},{24,8},{28,12},{1,17},{... | collective-permute-start | bytes 442376 | tf_op jit(solution)/shard_map/ppermute | solution.py:57
  91.8 10.3 %collective-permute-start.24 = (bf16[24,3072]{1,0:T(8,128)(2,1)}, bf16[24,3072]{1,0:T(8,128)(2,1)S(1)}, u32[]{:S(2)}, u32[]{:S(2)}) collective-permute-start(bf16[24,3072]{1,0:T(8,128)(2,1)} %fusion.91), channel_id=1, source_target_pairs={{0,24},{4,28},{8,16},{12,20},{16,8},{20,12},{24,0},{28,4},{1,25},{... | collective-permute-start | bytes 442376 | tf_op jit(solution)/shard_map/ppermute | solution.py:57
  100.5 11.0 %collective-permute-start.14 = (bf16[4,48,864]{2,1,0:T(8,128)(2,1)S(1)}, bf16[4,48,864]{2,1,0:T(8,128)(2,1)S(1)}, u32[]{:S(2)}, u32[]{:S(2)}) collective-permute-start(bf16[4,48,864]{2,1,0:T(8,128)(2,1)S(1)} %bitcast_dynamic-update-slice_fusion.12), channel_id=1, source_target_pairs={{0,4},{4,0},{8,12},{12,8},{16,20},{20,16},{24,28},{28,24},{1,5},{5... | collective-permute-start | bytes 995336 | tf_op jit(solution)/shard_map/ppermute | solution.py:57
  102.0 22.1 %collective-permute-start.19 = (bf16[4,24,3072]{2,1,0:T(8,128)(2,1)S(1)}, bf16[4,24,3072]{2,1,0:T(8,128)(2,1)S(1)}, u32[]{:S(2)}, u32[]{:S(2)}) collective-permute-start(bf16[4,24,3072]{2,1,0:T(8,128)(2,1)S(1)} %bitcast_dynamic-update-slice_fusion.8), channel_id=1, source_target_pairs={{0,4},{4,0},{8,12},{12,8},{16,20},{20,16},{24,28},{28,24},{1,5},{5... | collective-permute-start | bytes 1769480 | tf_op jit(solution)/shard_map/ppermute | solution.py:57
  102.7 34.1 %collective-permute-start.25 = (bf16[4,24,3072]{2,1,0:T(8,128)(2,1)S(1)}, bf16[4,24,3072]{2,1,0:T(8,128)(2,1)S(1)}, u32[]{:S(2)}, u32[]{:S(2)}) collective-permute-start(bf16[4,24,3072]{2,1,0:T(8,128)(2,1)S(1)} %bitcast_dynamic-update-slice_fusion.5), channel_id=1, source_target_pairs={{0,4},{4,0},{8,12},{12,8},{16,20},{20,16},{24,28},{28,24},{1,5},{5... | collective-permute-start | bytes 1769480 | tf_op jit(solution)/shard_map/ppermute | solution.py:57
  106.3 54.0 %collective-permute-start.9 = (bf16[4,48,3384]{2,1,0:T(8,128)(2,1)S(1)}, bf16[4,48,3384]{2,1,0:T(8,128)(2,1)S(1)}, u32[]{:S(2)}, u32[]{:S(2)}) collective-permute-start(bf16[4,48,3384]{2,1,0:T(8,128)(2,1)S(1)} %bitcast_dynamic-update-slice_fusion), channel_id=1, source_target_pairs={{0,4},{4,0},{8,12},{12,8},{16,20},{20,16},{24,28},{28,24},{1,5},{5... | collective-permute-start | bytes 3898376 | tf_op jit(solution)/shard_map/ppermute | solution.py:57
  111.7 49.3 %collective-permute-start.15 = (bf16[2,4,48,864]{3,2,0,1:T(8,128)(2,1)S(1)}, bf16[2,4,48,864]{3,2,0,1:T(8,128)(2,1)S(1)}, u32[]{:S(2)}, u32[]{:S(2)}) collective-permute-start(bf16[2,4,48,864]{3,2,0,1:T(8,128)(2,1)S(1)} %pad_maximum_fusion.11), channel_id=1, source_target_pairs={{0,1},{1,0},{2,3},{3,2},{4,5},{5,4},{6,7},{7,6},{8,9},{9,8},{10,11... | collective-permute-start | bytes 1990664 | tf_op jit(solution)/shard_map/ppermute | solution.py:57
  124.4 38.1 %collective-permute-start.20 = (bf16[2,4,24,3072]{3,2,0,1:T(8,128)(2,1)S(1)}, bf16[2,4,24,3072]{3,2,0,1:T(8,128)(2,1)S(1)}, u32[]{:S(2)}, u32[]{:S(2)}) collective-permute-start(bf16[2,4,24,3072]{3,2,0,1:T(8,128)(2,1)S(1)} %pad_maximum_fusion.9), channel_id=1, source_target_pairs={{0,2},{1,3},{2,0},{3,1},{4,6},{5,7},{6,4},{7,5},{8,10},{9,11},{10,... | collective-permute-start | bytes 3538952 | tf_op jit(solution)/shard_map/ppermute | solution.py:57
  137.0 30.9 %collective-permute-start.26 = (bf16[2,4,24,3072]{3,2,0,1:T(8,128)(2,1)S(1)}, bf16[2,4,24,3072]{3,2,0,1:T(8,128)(2,1)S(1)}, u32[]{:S(2)}, u32[]{:S(2)}) collective-permute-start(bf16[2,4,24,3072]{3,2,0,1:T(8,128)(2,1)S(1)} %pad_maximum_fusion.10), channel_id=1, source_target_pairs={{0,2},{1,3},{2,0},{3,1},{4,6},{5,7},{6,4},{7,5},{8,10},{9,11},{10,... | collective-permute-start | bytes 3538952 | tf_op jit(solution)/shard_map/ppermute | solution.py:57
  160.9 8.8 %collective-permute-start.10 = (bf16[2,4,48,3384]{3,2,0,1:T(8,128)(2,1)S(1)}, bf16[2,4,48,3384]{3,2,0,1:T(8,128)(2,1)S(1)}, u32[]{:S(2)}, u32[]{:S(2)}) collective-permute-start(bf16[2,4,48,3384]{3,2,0,1:T(8,128)(2,1)S(1)} %pad_maximum_fusion.2), channel_id=1, source_target_pairs={{0,1},{1,0},{2,3},{3,2},{4,5},{5,4},{6,7},{7,6},{8,9},{9,8},{10,11... | collective-permute-start | bytes 7796744 | tf_op jit(solution)/shard_map/ppermute | solution.py:57
  162.8 51.8 %collective-permute-start.21 = (bf16[2,2,4,24,3072]{4,3,0,1,2:T(8,128)(2,1)S(1)}, bf16[2,2,4,24,3072]{4,3,0,1,2:T(8,128)(2,1)}, u32[]{:S(2)}, u32[]{:S(2)}) collective-permute-start(bf16[2,2,4,24,3072]{4,3,0,1,2:T(8,128)(2,1)S(1)} %pad_maximum_fusion.4), channel_id=1, source_target_pairs={{0,1},{1,0},{2,3},{3,2},{4,5},{5,4},{6,7},{7,6},{8,9},{9,8},{10,11... | collective-permute-start | bytes 7077896 | tf_op jit(solution)/shard_map/ppermute | solution.py:57
  169.7 39.2 %collective-permute-start.27 = (bf16[2,2,4,24,3072]{4,3,0,1,2:T(8,128)(2,1)}, bf16[2,2,4,24,3072]{4,3,0,1,2:T(8,128)(2,1)}, u32[]{:S(2)}, u32[]{:S(2)}) collective-permute-start(bf16[2,2,4,24,3072]{4,3,0,1,2:T(8,128)(2,1)} %pad_maximum_fusion.5), channel_id=1, source_target_pairs={{0,1},{1,0},{2,3},{3,2},{4,5},{5,4},{6,7},{7,6},{8,9},{9,8},{10,11... | collective-permute-start | bytes 7077896 | tf_op jit(solution)/shard_map/ppermute | solution.py:57
  377.9 10.3 %collective-permute-start.58 = (f32[4,2,2,24,152]{4,3,2,1,0:T(8,128)S(1)}, f32[4,2,2,24,152]{4,3,2,1,0:T(8,128)S(1)}, u32[]{:S(2)}, u32[]{:S(2)}) collective-permute-start(f32[4,2,2,24,152]{4,3,2,1,0:T(8,128)S(1)} %dynamic-slice_bitcast_fusion), channel_id=1, source_target_pairs={{0,1},{1,0},{2,3},{3,2},{4,5},{5,4},{6,7},{7,6},{8,9},{9,8},{10,11... | collective-permute-start | bytes 700424 | tf_op jit(solution)/shard_map/ppermute | solution.py:71
  384.7 35.6 %collective-permute-start.52 = (bf16[4,2,2,24,1024]{4,3,2,1,0:T(8,128)(2,1)}, bf16[4,2,2,24,1024]{4,3,2,1,0:T(8,128)(2,1)}, u32[]{:S(2)}, u32[]{:S(2)}) collective-permute-start(bf16[4,2,2,24,1024]{4,3,2,1,0:T(8,128)(2,1)} %fusion.33), channel_id=1, source_target_pairs={{0,1},{1,0},{2,3},{3,2},{4,5},{5,4},{6,7},{7,6},{8,9},{9,8},{10,11... | collective-permute-start | bytes 2359304 | tf_op jit(solution)/shard_map/ppermute | solution.py:71
  388.3 7.3 %collective-permute-start.59 = (f32[4,2,24,152]{3,2,1,0:T(8,128)S(1)}, f32[4,2,24,152]{3,2,1,0:T(8,128)S(1)}, u32[]{:S(2)}, u32[]{:S(2)}) collective-permute-start(f32[4,2,24,152]{3,2,1,0:T(8,128)S(1)} %dynamic-slice_bitcast_fusion.1), channel_id=1, source_target_pairs={{0,4},{4,0},{8,12},{12,8},{16,20},{20,16},{24,28},{28,24},{1,5},{5... | collective-permute-start | bytes 350216 | tf_op jit(solution)/shard_map/ppermute | solution.py:71
  393.3 67.5 %collective-permute-start.46 = (bf16[4,2,2,24,2304]{4,3,2,1,0:T(8,128)(2,1)}, bf16[4,2,2,24,2304]{4,3,2,1,0:T(8,128)(2,1)}, u32[]{:S(2)}, u32[]{:S(2)}) collective-permute-start(bf16[4,2,2,24,2304]{4,3,2,1,0:T(8,128)(2,1)} %fusion.15), channel_id=1, source_target_pairs={{0,1},{1,0},{2,3},{3,2},{4,5},{5,4},{6,7},{7,6},{8,9},{9,8},{10,11... | collective-permute-start | bytes 5308424 | tf_op jit(solution)/shard_map/ppermute | solution.py:71
  395.6 5.6 collective-permute-start.60
  406.7 10.4 %collective-permute-start.40 = (bf16[4,2,2,24,768]{4,3,2,1,0:T(8,128)(2,1)}, bf16[4,2,2,24,768]{4,3,2,1,0:T(8,128)(2,1)}, u32[]{:S(2)}, u32[]{:S(2)}) collective-permute-start(bf16[4,2,2,24,768]{4,3,2,1,0:T(8,128)(2,1)} %fusion.44), channel_id=1, source_target_pairs={{0,1},{1,0},{2,3},{3,2},{4,5},{5,4},{6,7},{7,6},{8,9},{9,8},{10,11... | collective-permute-start | bytes 1769480 | tf_op jit(solution)/shard_map/ppermute | solution.py:71
  407.6 77.2 %collective-permute-start.34 = (bf16[4,2,2,24,3072]{4,3,0,1,2:T(8,128)(2,1)}, bf16[4,2,2,24,3072]{4,3,0,1,2:T(8,128)(2,1)}, u32[]{:S(2)}, u32[]{:S(2)}) collective-permute-start(bf16[4,2,2,24,3072]{4,3,0,1,2:T(8,128)(2,1)} %fusion.13), channel_id=1, source_target_pairs={{0,1},{1,0},{2,3},{3,2},{4,5},{5,4},{6,7},{7,6},{8,9},{9,8},{10,11... | collective-permute-start | bytes 7077896 | tf_op jit(solution)/shard_map/ppermute | solution.py:71
  410.7 6.3 collective-permute-start.64
  418.7 9.5 %collective-permute-start.41 = (bf16[4,2,24,768]{3,2,1,0:T(8,128)(2,1)S(1)}, bf16[4,2,24,768]{3,2,1,0:T(8,128)(2,1)S(1)}, u32[]{:S(2)}, u32[]{:S(2)}) collective-permute-start(bf16[4,2,24,768]{3,2,1,0:T(8,128)(2,1)S(1)} %fusion.56), channel_id=1, source_target_pairs={{0,4},{4,0},{8,12},{12,8},{16,20},{20,16},{24,28},{28,24},{1,5},{5... | collective-permute-start | bytes 884744 | tf_op jit(solution)/shard_map/ppermute | solution.py:71
  428.9 5.8 collective-permute-start.42
  431.2 10.6 %collective-permute-start.53 = (bf16[4,2,24,1024]{3,2,1,0:T(8,128)(2,1)}, bf16[4,2,24,1024]{3,2,1,0:T(8,128)(2,1)S(1)}, u32[]{:S(2)}, u32[]{:S(2)}) collective-permute-start(bf16[4,2,24,1024]{3,2,1,0:T(8,128)(2,1)} %fusion.47), channel_id=1, source_target_pairs={{0,4},{4,0},{8,12},{12,8},{16,20},{20,16},{24,28},{28,24},{1,5},{5... | collective-permute-start | bytes 1179656 | tf_op jit(solution)/shard_map/ppermute | solution.py:71
  435.7 9.0 %collective-permute-start.43 = (bf16[24,768]{1,0:T(8,128)(2,1)S(1)}, bf16[24,768]{1,0:T(8,128)(2,1)S(1)}, u32[]{:S(2)}, u32[]{:S(2)}) collective-permute-start(bf16[24,768]{1,0:T(8,128)(2,1)S(1)} %get-tuple-element.241), channel_id=1, source_target_pairs={{0,8},{4,12},{8,0},{12,4},{16,24},{20,28},{24,16},{28,20},{1,9},{5... | collective-permute-start | bytes 110600 | tf_op jit(solution)/shard_map/ppermute | solution.py:71
  435.9 9.4 %collective-permute-start.44 = (bf16[24,768]{1,0:T(8,128)(2,1)S(1)}, bf16[24,768]{1,0:T(8,128)(2,1)S(1)}, u32[]{:S(2)}, u32[]{:S(2)}) collective-permute-start(bf16[24,768]{1,0:T(8,128)(2,1)S(1)} %get-tuple-element.243), channel_id=1, source_target_pairs={{0,16},{4,20},{8,24},{12,28},{16,0},{20,4},{24,8},{28,12},{1,17},{... | collective-permute-start | bytes 110600 | tf_op jit(solution)/shard_map/ppermute | solution.py:71
  441.9 5.8 collective-permute-start.45
  444.7 6.4 collective-permute-start.54
  453.7 5.9 collective-permute-start.57
  455.7 40.7 %collective-permute-start.28 = (bf16[4,2,2,24,3072]{4,3,2,1,0:T(8,128)(2,1)S(1)}, bf16[4,2,2,24,3072]{4,3,2,1,0:T(8,128)(2,1)}, u32[]{:S(2)}, u32[]{:S(2)}) collective-permute-start(bf16[4,2,2,24,3072]{4,3,2,1,0:T(8,128)(2,1)S(1)} %copy-done.22), channel_id=1, source_target_pairs={{0,1},{1,0},{2,3},{3,2},{4,5},{5,4},{6,7},{7,6},{8,9},{9,8},{10,11... | collective-permute-start | bytes 7077896 | tf_op jit(solution)/shard_map/ppermute | solution.py:71
  464.1 18.9 %collective-permute-start.47 = (bf16[4,2,24,2304]{3,2,1,0:T(8,128)(2,1)S(1)}, bf16[4,2,24,2304]{3,2,1,0:T(8,128)(2,1)S(1)}, u32[]{:S(2)}, u32[]{:S(2)}) collective-permute-start(bf16[4,2,24,2304]{3,2,1,0:T(8,128)(2,1)S(1)} %fusion.30), channel_id=1, source_target_pairs={{0,2},{1,3},{2,0},{3,1},{4,6},{5,7},{6,4},{7,5},{8,10},{9,11},{10,... | collective-permute-start | bytes 2654216 | tf_op jit(solution)/shard_map/ppermute | solution.py:71
  483.3 8.5 %collective-permute-start.48 = (bf16[4,24,2304]{2,1,0:T(8,128)(2,1)S(1)}, bf16[4,24,2304]{2,1,0:T(8,128)(2,1)S(1)}, u32[]{:S(2)}, u32[]{:S(2)}) collective-permute-start(bf16[4,24,2304]{2,1,0:T(8,128)(2,1)S(1)} %fusion.45), channel_id=1, source_target_pairs={{0,4},{4,0},{8,12},{12,8},{16,20},{20,16},{24,28},{28,24},{1,5},{5... | collective-permute-start | bytes 1327112 | tf_op jit(solution)/shard_map/ppermute | solution.py:71
  488.4 29.5 %collective-permute-start.35 = (bf16[4,2,24,3072]{3,2,0,1:T(8,128)(2,1)S(1)}, bf16[4,2,24,3072]{3,2,0,1:T(8,128)(2,1)S(1)}, u32[]{:S(2)}, u32[]{:S(2)}) collective-permute-start(bf16[4,2,24,3072]{3,2,0,1:T(8,128)(2,1)S(1)} %fusion.22), channel_id=1, source_target_pairs={{0,2},{1,3},{2,0},{3,1},{4,6},{5,7},{6,4},{7,5},{8,10},{9,11},{10,... | collective-permute-start | bytes 3538952 | tf_op jit(solution)/shard_map/ppermute | solution.py:71
  492.0 7.1 %collective-permute-start.49 = (bf16[24,2304]{1,0:T(8,128)(2,1)S(1)}, bf16[24,2304]{1,0:T(8,128)(2,1)S(1)}, u32[]{:S(2)}, u32[]{:S(2)}) collective-permute-start(bf16[24,2304]{1,0:T(8,128)(2,1)S(1)} %get-tuple-element.223), channel_id=1, source_target_pairs={{0,8},{4,12},{8,0},{12,4},{16,24},{20,28},{24,16},{28,20},{1,9},{5... | collective-permute-start | bytes 331784 | tf_op jit(solution)/shard_map/ppermute | solution.py:71
  492.4 6.8 %collective-permute-start.50 = (bf16[24,2304]{1,0:T(8,128)(2,1)S(1)}, bf16[24,2304]{1,0:T(8,128)(2,1)S(1)}, u32[]{:S(2)}, u32[]{:S(2)}) collective-permute-start(bf16[24,2304]{1,0:T(8,128)(2,1)S(1)} %get-tuple-element.225), channel_id=1, source_target_pairs={{0,16},{4,20},{8,24},{12,28},{16,0},{20,4},{24,8},{28,12},{1,17},{... | collective-permute-start | bytes 331784 | tf_op jit(solution)/shard_map/ppermute | solution.py:71
  494.5 6.7 %collective-permute-start.51 = (bf16[24,2304]{1,0:T(8,128)(2,1)S(1)}, bf16[24,2304]{1,0:T(8,128)(2,1)S(1)}, u32[]{:S(2)}, u32[]{:S(2)}) collective-permute-start(bf16[24,2304]{1,0:T(8,128)(2,1)S(1)} %get-tuple-element.224), channel_id=1, source_target_pairs={{0,24},{4,28},{8,16},{12,20},{16,8},{20,12},{24,0},{28,4},{1,25},{... | collective-permute-start | bytes 331784 | tf_op jit(solution)/shard_map/ppermute | solution.py:71
  501.8 15.2 %collective-permute-start.68 = (f32[24,2304]{1,0:T(8,128)S(1)}, f32[24,2304]{1,0:T(8,128)S(1)}, u32[]{:S(2)}, u32[]{:S(2)}) collective-permute-start(f32[24,2304]{1,0:T(8,128)S(1)} %get-tuple-element.176), channel_id=1, source_target_pairs={{0,2},{1,3},{2,0},{3,1},{4,6},{5,7},{6,4},{7,5},{8,10},{9,11},{10,... | collective-permute-start | bytes 663560 | tf_op jit(solution)/shard_map/ppermute | solution.py:57
  503.5 25.0 %collective-permute-start.29 = (bf16[4,2,24,3072]{3,2,1,0:T(8,128)(2,1)S(1)}, bf16[4,2,24,3072]{3,2,1,0:T(8,128)(2,1)S(1)}, u32[]{:S(2)}, u32[]{:S(2)}) collective-permute-start(bf16[4,2,24,3072]{3,2,1,0:T(8,128)(2,1)S(1)} %fusion.21), channel_id=1, source_target_pairs={{0,4},{4,0},{8,12},{12,8},{16,20},{20,16},{24,28},{28,24},{1,5},{5... | collective-permute-start | bytes 3538952 | tf_op jit(solution)/shard_map/ppermute | solution.py:71
  517.9 48.7 %collective-permute-start.69 = (f32[2,24,2304]{2,1,0:T(8,128)}, f32[2,24,2304]{2,1,0:T(8,128)}, u32[]{:S(2)}, u32[]{:S(2)}) collective-permute-start(f32[2,24,2304]{2,1,0:T(8,128)} %pad_maximum_fusion.14), channel_id=1, source_target_pairs={{0,1},{1,0},{2,3},{3,2},{4,5},{5,4},{6,7},{7,6},{8,9},{9,8},{10,11... | collective-permute-start | bytes 1327112 | tf_op jit(solution)/shard_map/ppermute | solution.py:57
  518.4 19.2 %collective-permute-start.36 = (bf16[4,24,3072]{2,1,0:T(8,128)(2,1)S(1)}, bf16[4,24,3072]{2,1,0:T(8,128)(2,1)S(1)}, u32[]{:S(2)}, u32[]{:S(2)}) collective-permute-start(bf16[4,24,3072]{2,1,0:T(8,128)(2,1)S(1)} %fusion.43), channel_id=1, source_target_pairs={{0,4},{4,0},{8,12},{12,8},{16,20},{20,16},{24,28},{28,24},{1,5},{5... | collective-permute-start | bytes 1769480 | tf_op jit(solution)/shard_map/ppermute | solution.py:71
  528.9 13.3 %collective-permute-start.30 = (bf16[4,24,3072]{2,1,0:T(8,128)(2,1)S(1)}, bf16[4,24,3072]{2,1,0:T(8,128)(2,1)S(1)}, u32[]{:S(2)}, u32[]{:S(2)}) collective-permute-start(bf16[4,24,3072]{2,1,0:T(8,128)(2,1)S(1)} %fusion.42), channel_id=1, source_target_pairs={{0,2},{1,3},{2,0},{3,1},{4,6},{5,7},{6,4},{7,5},{8,10},{9,11},{10,... | collective-permute-start | bytes 1769480 | tf_op jit(solution)/shard_map/ppermute | solution.py:71
  537.8 9.5 %collective-permute-start.37 = (bf16[24,3072]{1,0:T(8,128)(2,1)S(1)}, bf16[24,3072]{1,0:T(8,128)(2,1)S(1)}, u32[]{:S(2)}, u32[]{:S(2)}) collective-permute-start(bf16[24,3072]{1,0:T(8,128)(2,1)S(1)} %get-tuple-element.211), channel_id=1, source_target_pairs={{0,8},{4,12},{8,0},{12,4},{16,24},{20,28},{24,16},{28,20},{1,9},{5... | collective-permute-start | bytes 442376 | tf_op jit(solution)/shard_map/ppermute | solution.py:71
  539.5 14.0 %collective-permute-start.38 = (bf16[24,3072]{1,0:T(8,128)(2,1)S(1)}, bf16[24,3072]{1,0:T(8,128)(2,1)S(1)}, u32[]{:S(2)}, u32[]{:S(2)}) collective-permute-start(bf16[24,3072]{1,0:T(8,128)(2,1)S(1)} %get-tuple-element.213), channel_id=1, source_target_pairs={{0,16},{4,20},{8,24},{12,28},{16,0},{20,4},{24,8},{28,12},{1,17},{... | collective-permute-start | bytes 442376 | tf_op jit(solution)/shard_map/ppermute | solution.py:71
  540.3 15.2 %collective-permute-start.39 = (bf16[24,3072]{1,0:T(8,128)(2,1)S(1)}, bf16[24,3072]{1,0:T(8,128)(2,1)S(1)}, u32[]{:S(2)}, u32[]{:S(2)}) collective-permute-start(bf16[24,3072]{1,0:T(8,128)(2,1)S(1)} %get-tuple-element.212), channel_id=1, source_target_pairs={{0,24},{4,28},{8,16},{12,20},{16,8},{20,12},{24,0},{28,4},{1,25},{... | collective-permute-start | bytes 442376 | tf_op jit(solution)/shard_map/ppermute | solution.py:71
  542.4 13.7 %collective-permute-start.31 = (bf16[24,3072]{1,0:T(8,128)(2,1)S(1)}, bf16[24,3072]{1,0:T(8,128)(2,1)S(1)}, u32[]{:S(2)}, u32[]{:S(2)}) collective-permute-start(bf16[24,3072]{1,0:T(8,128)(2,1)S(1)} %get-tuple-element.214), channel_id=1, source_target_pairs={{0,8},{4,12},{8,0},{12,4},{16,24},{20,28},{24,16},{28,20},{1,9},{5... | collective-permute-start | bytes 442376 | tf_op jit(solution)/shard_map/ppermute | solution.py:71
  547.3 14.7 %collective-permute-start.32 = (bf16[24,3072]{1,0:T(8,128)(2,1)S(1)}, bf16[24,3072]{1,0:T(8,128)(2,1)S(1)}, u32[]{:S(2)}, u32[]{:S(2)}) collective-permute-start(bf16[24,3072]{1,0:T(8,128)(2,1)S(1)} %get-tuple-element.216), channel_id=1, source_target_pairs={{0,16},{4,20},{8,24},{12,28},{16,0},{20,4},{24,8},{28,12},{1,17},{... | collective-permute-start | bytes 442376 | tf_op jit(solution)/shard_map/ppermute | solution.py:71
  553.5 8.5 %collective-permute-start.33 = (bf16[24,3072]{1,0:T(8,128)(2,1)S(1)}, bf16[24,3072]{1,0:T(8,128)(2,1)S(1)}, u32[]{:S(2)}, u32[]{:S(2)}) collective-permute-start(bf16[24,3072]{1,0:T(8,128)(2,1)S(1)} %get-tuple-element.215), channel_id=1, source_target_pairs={{0,24},{4,28},{8,16},{12,20},{16,8},{20,12},{24,0},{28,4},{1,25},{... | collective-permute-start | bytes 442376 | tf_op jit(solution)/shard_map/ppermute | solution.py:71
  608.6 18.8 %collective-permute-start.74 = (f32[24,3072]{1,0:T(8,128)S(1)}, f32[24,3072]{1,0:T(8,128)}, u32[]{:S(2)}, u32[]{:S(2)}) collective-permute-start(f32[24,3072]{1,0:T(8,128)S(1)} %get-tuple-element.182), channel_id=1, source_target_pairs={{0,2},{1,3},{2,0},{3,1},{4,6},{5,7},{6,4},{7,5},{8,10},{9,11},{10,... | collective-permute-start | bytes 884744 | tf_op jit(solution)/shard_map/ppermute | solution.py:57
  611.1 17.4 %collective-permute-start.72 = (f32[24,3072]{1,0:T(8,128)S(1)}, f32[24,3072]{1,0:T(8,128)}, u32[]{:S(2)}, u32[]{:S(2)}) collective-permute-start(f32[24,3072]{1,0:T(8,128)S(1)} %get-tuple-element.180), channel_id=1, source_target_pairs={{0,2},{1,3},{2,0},{3,1},{4,6},{5,7},{6,4},{7,5},{8,10},{9,11},{10,... | collective-permute-start | bytes 884744 | tf_op jit(solution)/shard_map/ppermute | solution.py:57
  (97 other events, 1118.6 us)

commit v2 on v1

--- a/solution.py
+++ b/solution.py
@@ -23,6 +23,27 @@
 F32 = jnp.float32
 BF16 = jnp.bfloat16
 WIRE = jnp.bfloat16
+GATHER = [
+    (1, 0, 1536, True),
+    (1, 1536, 1536, True),
+    (2, 0, 1536, True),
+    (2, 1536, 1536, True),
+    (3, 0, 768, True),
+    (0, 0, 2304, False),
+    (4, 0, 1024, False),
+    (5, 0, 256, False),
+]
+REDUCE = [
+    (5, 0, 256, "xy"),
+    (0, 0, 1536, "yx"),
+    (0, 1536, 1536, "xy"),
+    (1, 0, 1536, "yx"),
+    (1, 1536, 1536, "xy"),
+    (2, 0, 768, "yx"),
+    (3, 0, 1280, "xy"),
+    (3, 1280, 1024, "yx"),
+    (4, 0, 1024, "xy"),
+]
 NN = (((1,), (0,)), ((), ()))
 NT = (((1,), (1,)), ((), ()))
 TN = (((0,), (0,)), ((), ()))
@@ -117,6 +138,248 @@
     part = gather_line(part, ways["y"])
     part = gather_line(part, ways["core"])
     return part.reshape(-1, part.shape[-1])
+
+
+MESH=pl.DeviceIdType.MESH
+X = 2
+Z = 4
+def here():
+    d=lax.axis_index("dp"); s=lax.axis_index("seq")
+    return d//X, d%X, s//2, s%2
+def peer(kz,kx,ky,kc):
+    z,x,y,c=here()
+    return ((z^kz)*X+(x^kx), (y^ky)*2+(c^kc))
+class Gather:
+    def __init__(s, src, dst, sems, base, split, lo, width):
+        s.src,s.dst,s.split,s.lo,s.width=src,dst,split,lo,width
+        s.send,s.recv=sems; s.n=base
+        s.live=[]; s.rows=src.shape[0]
+        s.idx={}
+    def region(s,ref,kz,kx,half,ky,local=False):
+        z,x,y,c=here(); r=s.rows//2
+        row=(c^half)*r
+        if not local: row=row+((z^kz)*X+(x^kx))*s.rows
+        row=pl.multiple_of(row,16)
+        if ky is None: return ref.at[pl.ds(row,r),pl.ds(s.lo,s.width)]
+        w=s.width//2
+        return ref.at[pl.ds(row,r),pl.ds(pl.multiple_of(s.lo+(y^ky)*w,128),w)]
+    def copy(s,key,kz,kx,ky,to,own=False):
+        i=s.idx.setdefault(key,s.n)
+        if i==s.n: s.n+=1
+        col=ky if s.split else None
+        return pltpu.make_async_remote_copy(s.region(s.src if own else s.dst,kz,kx,0,col,own),s.region(s.dst,kz,kx,0,col),s.send.at[i],s.recv.at[i],device_id=peer(*to),device_id_type=MESH)
+    def start(s,*a,**k):
+        c=s.copy(*a,**k); c.start(); s.live.append(c); return c
+    def begin(s):
+        for k in (1,2,3): s.start(("z",k),0,0,0,(k,0,0,0),own=True)
+        s.start(("x",0),0,0,0,(0,1,0,0),own=True)
+    def after_z(s,k):
+        s.recvd(("z",k),k,0,0)
+        s.start(("x",k),k,0,0,(0,1,0,0))
+        if s.split: s.start(("y",k,0),k,0,0,(0,0,1,0))
+        s.start(("c",k,0),k,0,0,(0,0,0,1))
+    def after_x(s,k):
+        s.recvd(("x",k),k,1,0)
+        if s.split: s.start(("y",k,1),k,1,0,(0,0,1,0))
+        s.start(("c",k,1),k,1,0,(0,0,0,1))
+    def after_y(s,k,kx):
+        s.recvd(("y",k,kx),k,kx,1)
+        s.start(("d",k,kx),k,kx,1,(0,0,0,1))
+    def recvd(s,key,kz,kx,ky):
+        s.copy(key,kz,kx,ky,(0,0,0,1)).wait_recv()
+    def stage_z(s):
+        for k in (1,2,3): s.after_z(k)
+    def stage_x(s):
+        for k in range(4): s.after_x(k)
+    def stage_y(s):
+        if s.split:
+            for kx in range(2):
+                for k in range(4):
+                    if k or kx: s.after_y(k,kx)
+    def finish(s):
+        for k in range(4):
+            for kx in range(2):
+                if (k or kx):
+                    s.core_recv(("c",k,kx),k,kx,0)
+                    if s.split: s.core_recv(("d",k,kx),k,kx,1)
+        for c in s.live: c.wait_send()
+    def core_recv(s,key,kz,kx,ky):
+        i=s.idx[key]; col=ky if s.split else None
+        r=s.region(s.dst,kz,kx,1,col)
+        pltpu.make_async_remote_copy(r,r,s.send.at[i],s.recv.at[i],device_id=peer(0,0,0,1),device_id_type=MESH).wait_recv()
+
+def greet(peers):
+    bar=pltpu.get_barrier_semaphore()
+    for p in peers: pl.semaphore_signal(bar,inc=1,device_id=peer(*p),device_id_type=MESH)
+    pl.semaphore_wait(bar,len(peers))
+PEERS=[(1,0,0,0),(2,0,0,0),(3,0,0,0),(0,1,0,0),(0,0,1,0),(0,0,0,1)]
+def gather_kernel(chunks,n,ahead,*refs):
+    src,dst=refs[:n],refs[n:2*n]; send,recv,loc=refs[2*n:]
+    greet(PEERS)
+    z,x,y,c=here()
+    mine=[]
+    for i in range(n):
+        r=src[i].shape[0]
+        m=pltpu.make_async_copy(src[i],dst[i].at[pl.ds(pl.multiple_of((z*X+x)*r,16),r),:],loc.at[i]); m.start(); mine.append(m)
+    g=[]; base=0
+    for (t,lo,w,sp) in chunks:
+        g.append(Gather(src[t],dst[t],(send,recv),base,sp,lo,w)); base+=28 if sp else 14
+    m=len(g)
+    for i in range(min(ahead,m)): g[i].begin()
+    for s in range(m+2):
+        if s<m:
+            g[s].stage_z()
+            if s+ahead<m: g[s+ahead].begin()
+        if 0<=s-1<m: g[s-1].stage_x()
+        if 0<=s-2<m: g[s-2].stage_y()
+    for a in g: a.finish()
+    for a in mine: a.wait()
+def gather(shards,chunks,ahead=2,cid=1):
+    n=len(shards); dp=lax.axis_size("dp")
+    tot=sum(28 if s[3] else 14 for s in chunks)
+    anyspec=pl.BlockSpec(memory_space=pl.ANY)
+    return pl.pallas_call(functools.partial(gather_kernel,chunks,n,ahead),
+      out_shape=[jax.ShapeDtypeStruct((s.shape[0]*dp,s.shape[1]),s.dtype) for s in shards],
+      in_specs=[pl.BlockSpec(memory_space=pltpu.VMEM)]*n,out_specs=[anyspec]*n,
+      scratch_shapes=[pltpu.SemaphoreType.DMA((tot,)),pltpu.SemaphoreType.DMA((tot,)),pltpu.SemaphoreType.DMA((n,))],
+      compiler_params=pltpu.CompilerParams(collective_id=cid,has_side_effects=True))(*shards)
+
+
+PER=8
+class Reduce:
+    def __init__(s,g,out,bufs,sems,base,lo,w,order):
+        s.g,s.out,s.lo,s.w,s.order=g,out,lo,w,order
+        s.gc,s.r1,s.p2,s.r2,s.p3,s.r3,s.p4,s.r4=bufs
+        s.send,s.recv,s.loc=sems; s.base=base; s.r=g.shape[3]
+    def col(s,ky,lo=0):
+        z,x,y,c=here(); h=s.w//2
+        return pl.ds(pl.multiple_of(lo+(y^ky)*h,128),h)
+    def remote(s,src,dst,i,to):
+        return pltpu.make_async_remote_copy(src,dst,s.send.at[s.base+i],s.recv.at[s.base+i],device_id=peer(*to),device_id_type=MESH)
+    def load(s):
+        z,x,y,c=here()
+        return pltpu.make_async_copy(s.g.at[:,:,c,:,pl.ds(s.lo,s.w)],s.gc,s.loc)
+    def c1(s):
+        z,x,y,c=here()
+        return s.remote(s.g.at[:,:,1-c,:,pl.ds(s.lo,s.w)],s.r1,0,(0,0,0,1))
+    def begin(s):
+        s.load().start(); s.c1().start()
+    def two(s,zz,xx,cols):
+        return s.gc[zz,xx,:,cols].astype(F32)+s.r1[zz,xx,:,cols].astype(F32)
+    def three(s,zz,xx,ky):
+        z,x,y,c=here()
+        if s.order=="xy": return s.two(zz,xx,s.col(ky))+s.r2[zz,:,s.col(ky)].astype(F32)
+        return s.two(zz,xx,s.col(ky))+s.r2[zz,xx].astype(F32)
+    def four(s,zz):
+        z,x,y,c=here()
+        return s.three(zz,x,0)+s.r3[zz].astype(F32)
+    def c2(s): return s.remote(s.p2,s.r2,1,(0,1,0,0) if s.order=="xy" else (0,0,1,0))
+    def c3(s): return s.remote(s.p3,s.r3,2,(0,0,1,0) if s.order=="xy" else (0,1,0,0))
+    def c4(s,k): return s.remote(s.p4.at[k-1],s.r4.at[k-1],2+k,(k,0,0,0))
+    def c5(s):
+        z,x,y,c=here()
+        ref=s.out.at[pl.ds(pl.multiple_of(c*s.r,8),s.r),s.col(0,s.lo)]
+        return s.remote(ref,ref,6,(0,0,1,0))
+    def c6(s):
+        z,x,y,c=here()
+        ref=s.out.at[pl.ds(pl.multiple_of(c*s.r,8),s.r),pl.ds(s.lo,s.w)]
+        return s.remote(ref,ref,7,(0,0,0,1))
+    def stage1(s):
+        z,x,y,c=here()
+        s.load().wait(); s.c1().wait_recv()
+        @pl.loop(0,Z)
+        def _(zz):
+            if s.order=="xy":
+                s.p2[zz]=s.two(zz,1-x,slice(None)).astype(s.p2.dtype)
+            else:
+                for xx in range(X): s.p2[zz,xx]=s.two(zz,xx,s.col(1)).astype(s.p2.dtype)
+        s.c2().start()
+    def stage2(s):
+        z,x,y,c=here()
+        s.c2().wait_recv()
+        @pl.loop(0,Z)
+        def _(zz):
+            s.p3[zz]=(s.three(zz,x,1) if s.order=="xy" else s.three(zz,1-x,0)).astype(s.p3.dtype)
+        s.c3().start()
+    def stage3(s):
+        z,x,y,c=here()
+        s.c3().wait_recv()
+        for k in (1,2,3):
+            s.p4[k-1]=s.four(z^k).astype(s.p4.dtype)
+            s.c4(k).start()
+    def stage4(s):
+        z,x,y,c=here()
+        total=s.four(z)
+        for k in (1,2,3):
+            s.c4(k).wait_recv()
+            total=total+s.r4[k-1].astype(F32)
+        s.out[pl.ds(pl.multiple_of(c*s.r,8),s.r),s.col(0,s.lo)]=total
+        s.c5().start()
+        return total
+    def stage5(s):
+        s.c5().wait_recv()
+        s.c6().start()
+    def finish(s):
+        s.c6().wait_recv()
+        s.c1().wait_send(); s.c2().wait_send(); s.c3().wait_send()
+        for k in (1,2,3): s.c4(k).wait_send()
+        s.c5().wait_send(); s.c6().wait_send()
+
+def shapes(r,w,order,dt):
+    h=w//2
+    two=(Z,r,w) if order=="xy" else (Z,X,r,h)
+    return [((Z,X,r,w),dt)]*2+[(two,dt)]*2+[((Z,r,h),dt)]*2+[((3,r,h),dt)]*2
+
+def totals(part,got,send,recv,base):
+    d=lax.axis_index("dp"); q=lax.axis_index("seq")
+    def hop(first,count,mine,peers):
+        got[first+mine]=part[...]
+        cs=[pltpu.make_async_remote_copy(part,got.at[first+mine],send.at[base+first+i],recv.at[base+first+i],device_id=p,device_id_type=MESH) for i,p in enumerate(peers)]
+        for k in cs: k.start()
+        for k in cs: k.wait()
+        t=got[first]
+        for i in range(1,count): t=t+got[first+i]
+        part[...]=t
+    hop(0,4,q,[peer(0,0,ky,kc) for ky,kc in ((0,1),(1,0),(1,1))])
+    hop(4,8,d,[peer(kz,kx,0,0) for kz,kx in ((0,1),(1,0),(1,1),(2,0),(2,1),(3,0),(3,1))])
+
+ALL=[(0,0,ky,kc) for ky,kc in ((0,1),(1,0),(1,1))]+[(kz,kx,0,0) for kz,kx in ((0,1),(1,0),(1,1),(2,0),(2,1),(3,0),(3,1))]
+def fold(v):
+    v=v*v
+    t=jnp.zeros((8,128),F32)
+    for i in range(v.shape[0]//8):
+        for j in range(v.shape[1]//128):
+            t=t+v[8*i:8*i+8,128*j:128*j+128]
+    return t
+def rs_kernel(chunks,n,*refs):
+    g,part=refs[:n],refs[n]
+    out,tot=refs[n+1:2*n+1],refs[2*n+1]
+    k=2*n+2
+    bufs=refs[k:k+8*len(chunks)]; send,recv,loc,got=refs[k+8*len(chunks):]
+    greet(ALL)
+    R=[Reduce(g[t],out[t],bufs[8*i:8*i+8],(send,recv,loc.at[i]),PER*i,lo,w,o) for i,(t,lo,w,o) in enumerate(chunks)]
+    m=len(R)
+    for a in R: a.begin()
+    tot[...]=part[...]
+    for s in range(m+4):
+        if s<m: R[s].stage1()
+        if 0<=s-1<m: R[s-1].stage2()
+        if 0<=s-2<m: R[s-2].stage3()
+        if 0<=s-3<m: tot[0]+=fold(R[s-3].stage4())
+        if 0<=s-4<m: R[s-4].stage5()
+    totals(tot,got,send,recv,PER*m)
+    for a in R: a.finish()
+def reduce_all(grads,part,chunks,cid=2):
+    n=len(grads); dp=lax.axis_size("dp")
+    r=grads[0].shape[0]//dp//2
+    anyspec=pl.BlockSpec(memory_space=pl.ANY); vm=pl.BlockSpec(memory_space=pltpu.VMEM)
+    bufs=[pltpu.VMEM(sh,dt) for (t,lo,w,o) in chunks for sh,dt in shapes(r,w,o,grads[t].dtype)]
+    ns=PER*len(chunks)+12
+    return pl.pallas_call(functools.partial(rs_kernel,chunks,n),
+      out_shape=[jax.ShapeDtypeStruct((2*r,g.shape[1]),F32) for g in grads]+[jax.ShapeDtypeStruct((3,8,128),F32)],
+      in_specs=[anyspec]*n+[vm],out_specs=[vm]*(n+1),
+      scratch_shapes=bufs+[pltpu.SemaphoreType.DMA((ns,)),pltpu.SemaphoreType.DMA((ns,)),pltpu.SemaphoreType.DMA((len(chunks),)),pltpu.VMEM((12,3,8,128),F32)],
+      compiler_params=pltpu.CompilerParams(collective_id=cid,has_side_effects=True,vmem_limit_bytes=60*2**20))(*[g.reshape(Z,X,2,r,-1) for g in grads],part)
 
 
 def visible(seg_key, seg_query, pos_query, keys, tile):
@@ -320,18 +583,24 @@
     part = lambda value: lax.dynamic_slice_in_dim(value, start, count, 0)
 
     low = lambda value: value.astype(BF16)
-    early = jnp.concatenate(
-        [low(attn_qkv), low(pos_table).T, low(embed_in).T, low(vectors).T], axis=1
+    outs = head_out.shape[1]
+    pad = lambda value, columns: jnp.pad(value, ((0, 0), (0, columns - value.shape[1])))
+    small = jnp.concatenate(
+        [
+            pad(low(head_out), 128),
+            pad(jnp.concatenate([low(embed_in).T, low(vectors).T], axis=1), 128),
+        ],
+        axis=1,
     )
-    early = gather_rows(early, ways, False)
-    w_qkv = early[:, : 3 * width]
-    w_pos = early[:, 3 * width : 3 * width + length + PATCH]
-    gains = early[:, 3 * width + length + PATCH :].astype(F32).T
-    w_attn = gather_rows(jnp.concatenate([low(attn_out), low(head_out)], axis=1), ways, False)
-    w_head = w_attn[:, width:]
-    w_attn = w_attn[:, :width]
-    w_up = gather_rows(low(mlp_up), ways, True)
-    w_down = gather_rows(low(mlp_down).T, ways, True)
+    shards = [low(attn_qkv), low(mlp_up), low(mlp_down).T, low(attn_out), low(pos_table).T, small]
+    aligned = (lax.axis_size("dp"), n_seq) == (X * Z, 4) and width % (32 * X * Z) == 0
+    if aligned:
+        w_qkv, w_up, w_down, w_attn, w_pos, w_small = gather(shards, GATHER)
+    else:
+        w_qkv, w_up, w_down, w_attn, w_pos, w_small = [gather_rows(v, ways, False) for v in shards]
+    w_head = w_small[:, :outs]
+    w_pos = jnp.concatenate([w_pos, w_small[:, 128 : 128 + PATCH]], axis=1)
+    gains = w_small[:, 128 + PATCH : 136 + PATCH].astype(F32).T
 
     at = jnp.arange(length)
     begins = jnp.zeros((length,), jnp.int32)
@@ -422,29 +691,33 @@
         axis=1,
     )
 
-    parts = [
-        scatter_rows(grad_down, ways, "xy", WIRE),
-        scatter_rows(grad_up, ways, "yx", WIRE),
-        scatter_rows(grad_attn, ways, "xy", WIRE),
-        scatter_rows(grad_qkv, ways, "yx", WIRE),
-        scatter_rows(grad_pos[:, :length], ways, "xy", WIRE),
-        scatter_rows(
-            jnp.concatenate([grad_head, grad_pos[:, length:], grad_vec], axis=1), ways, "xy", F32
-        ),
-    ]
-    squares = sum(jnp.sum(p * p) for p in parts)
-    squares, total, valid = lax.psum((squares, total, valid), ("dp", "seq"))
-    down, up, attn, wide, table, small = [gather_parts(p, ways) for p in parts]
-    outs = head_out.shape[1]
+    small = jnp.concatenate(
+        [pad(grad_head, 128), pad(jnp.concatenate([grad_pos[:, length:], grad_vec], axis=1), 128)],
+        axis=1,
+    )
+    grads = [low(grad_down), low(grad_up), low(grad_attn), low(grad_qkv), low(grad_pos[:, :length]), small]
+    if aligned:
+        part = jnp.zeros((3, 8, 128), F32).at[1, 0, 0].set(total).at[2, 0, 0].set(valid)
+        *sums, part = reduce_all(grads, part, REDUCE)
+        squares, total, valid = [jnp.sum(part[i]) for i in range(3)]
+    else:
+        parts = [
+            scatter_rows(g.astype(F32), ways, order, F32 if g is small else BF16)
+            for g, order in zip(grads, ("xy", "yx") * 3)
+        ]
+        squares = sum(jnp.sum(p * p) for p in parts)
+        squares, total, valid = lax.psum((squares, total, valid), ("dp", "seq"))
+        sums = [gather_parts(p, ways) for p in parts]
+    down, up, attn, wide, table, small = sums
     pieces = [
-        small[:, outs : outs + PATCH].T,
+        small[:, 128 : 128 + PATCH].T,
         table.T,
         wide,
         attn,
         up,
         down.T,
         small[:, :outs],
-        small[:, outs + PATCH :].T,
+        small[:, 128 + PATCH : 136 + PATCH].T,
     ]
     norm = jnp.sqrt(squares) / valid
     clip = jnp.minimum(1.0, CLIP_AT / (norm + 1e-06))

time: 653 us -> 478 us (0.73)
  Pallas kernels: 60.8 us -> 255 us
  waiting for transfers between devices: 174 us -> 0.02 us
  starting transfers between devices: 82.9 us -> 6.82 us
  blocking collectives: 40.1 us -> 0 us
  other arithmetic: 93.8 us -> 60.9 us
  local copies, waits for them, and re-layouts: 78.8 us -> 46 us
    pallas_call x0 -> x2, Pallas kernels: none -> 194 us  [the longest x1 118 us: reduce_all(): pl.pallas_call(functools.partial(rs_kernel, chunks, n), out_shape=[jax.Sh...]
    ppermute x70 -> x0, waiting for transfers between devices: 174 us -> none  [the longest x34 95.3 us: gather_line(): others = [lax.ppermute(block, axis, swap) for axis, swap in swaps]]
    ppermute x70 -> x0, starting transfers between devices: 79.1 us -> none  [the longest x34 39.7 us: gather_line(): others = [lax.ppermute(block, axis, swap) for axis, swap in swaps]]
    psum x1 -> x0, blocking collectives: 40.1 us -> none  [body(): squares, total, valid = lax.psum((squares, total, valid), ('dp', 'seq'))]
    another operation x40 -> x1, other arithmetic: 16.7 us -> 0.06 us  [the longest x38 16 us: gather_line(): jnp.stack([jnp.where(first, block, others[0]), jnp.where(first, others[0]...]
    convert_element_type x20 -> x3, local copies, waits for them, and re-layouts: 17.3 us -> 1.85 us  [body(): low = lambda value: value.astype(BF16)]
    add x18 -> x1, other arithmetic: 15.8 us -> 2.26 us  [adamw(): jnp.sqrt(second_hat) + ADAM_EPS]
    dynamic_update_slice x15 -> x0, local copies, waits for them, and re-layouts: 9.22 us -> none  [gather_line(): whole = lax.dynamic_update_index_in_dim(whole, piece, place ^ step, 0)]
  transfers between devices with their start and end apart: 76 -> 6, of which waited for: 33 -> 0; matrix products, arithmetic and copies ran while one was open for 20% -> 5% of each run, Pallas kernels for 3% -> 16%
where the time goes in v2:
time: 478 us; the launch traced here: 472 us
  Pallas kernels  255 us (53%)
  matrix products  94.5 us (20%)
  other arithmetic  60.9 us (13%)
  local copies, waits for them, and re-layouts  46 us (10%)
  between operations  8.82 us (2%)
  starting transfers between devices  6.82 us (1%)
    pallas_call x1, Pallas kernels, reduce_all(): pl.pallas_call(functools.partial(rs_kernel, chunks, n), out_shape=[jax.Sh...  118 us
    dot_general x18, matrix products, dot(): return lax.dot_general(left, right, dims, preferred_element_type=F32)  94.5 us
    pallas_call x1, Pallas kernels, gather(): pl.pallas_call(functools.partial(gather_kernel, chunks, n, ahead), out_sh...  76.3 us
    pallas_call x1, Pallas kernels, attend_back(): pl.pallas_call(functools.partial(attend_back_kernel, min(256, count), cou...  37.9 us
    pallas_call x1, Pallas kernels, attend(): pl.pallas_call(functools.partial(attend_kernel, min(256, count), count ==...  22.6 us
    sub x8, other arithmetic, adamw(): weight - rate * (first_hat / (jnp.sqrt(second_hat) + ADAM_EPS) + decay *...  20.2 us
    unnamed x178, local copies, waits for them, and re-layouts  18.6 us
    reduce_sum x3, other arithmetic, norm_back(): return (dhid, jnp.sum(grad * unit, 0), jnp.sum(grad, 0))  11.2 us
  transfers between devices with their start and end apart: 6, of which 0 were waited for; matrix products, arithmetic and copies ran while one was open for 5% of the time, Pallas kernels for 16%

profile of v2, /device:TPU:0, one launch (start us, length us, event | category | flops | bytes accessed | tf_op | source)
XLA Modules:
  0.0 471.6 jit_solution(5124289449470148758)
XLA Ops:
  2.0 2.5 collective-permute-start.1
  5.7 1.9 collective-permute-start.4
  7.6 2.2 convert_bitcast_fusion.refs_2_
  9.7 2.2 convert_element_type.141.refs_1_
  15.1 76.3 %shard_map.457 = (bf16[768,2304]{1,0:T(8,128)(2,1)}, bf16[768,3072]{1,0:T(8,128)(2,1)}, bf16[768,3072]{1,0:T(8,128)(2,1)}, bf16[768,768]{1,0:T(8,128)(2,1)}, bf1...) custom-call(bf16[96,2304]{1,0:T(8,128)(2,1)} %convert_element_type.140.refs_0_, ...), custom_call_target="tpu_custom_call" | custom-call | tf_op jit(solution)/shard_map/pallas_call | solution.py:241
  91.3 1.1 convert_bitcast_fusion.1
  92.5 1.6 slice_reduce_fusion
  98.6 1.1 dynamic_update_slice.30
  99.7 1.7 collective-permute-start.5
  102.5 3.2 select_subtract_fusion
  106.1 3.4 fusion.77
  112.1 1.1 dynamic_update_slice.31
  113.2 1.1 dynamic_update_slice.32
  114.4 1.1 dynamic_update_slice.33
  115.6 0.8 copy.129
  116.4 3.9 add_reduce_fusion
  120.9 6.1 %convolution_convert_fusion.q_ref.k_ref.v_ref = bf16[1024,2304]{1,0:T(8,128)(2,1)} fusion(bf16[768,2304]{1,0:T(8,128)(2,1)S(1)} %copy-done.66, f32[768]{0:T(1024)S(1)} %get-tuple-element.182, f32[768]{0:T(1024)S(1)} %get-tuple-element.183, f32[1024]{0:T(1024)S(1)} %add_rsqrt_fusion.2, f32[1024]{0:T(1024)S(1)} %broadcast_multiply_fusion.11, ...), kind=kOutput, calls=%fused_computation.10 | convolution fusion | flops 3630956544 | bytes 11420672 | tf_op jit(solution)/shard_map/dot_general | solution.py:53
  127.0 22.6 %shard_map.458 = (bf16[1024,768]{1,0:T(8,128)(2,1)S(1)}, f32[6,2,1024]{2,1,0:T(2,128)S(1)}) custom-call(bf16[1024,2304]{1,0:T(8,128)(2,1)} %convolution_convert_fusion.q_ref.k_ref.v_ref, bf16[1024,2304]{1,0:T(8,128)(2,1)} %convolution_convert_fusion.q_ref.k_ref.v_ref, bf16[1024,2304]{1,0:T(8,128)(2,1)} %convolution_convert_fusion.q_ref.k_ref.v_ref, ...), custom_call_target="tpu_custom_call" | custom-call | flops 24999999488 | bytes 8000000 | tf_op jit(solution)/shard_map/pallas_call | solution.py:455
  149.7 1.7 fusion.79
  152.9 5.4 %fusion.61 = f32[1024,3072]{1,0:T(8,128)S(1)} fusion(bf16[768,3072]{1,0:T(8,128)(2,1)S(1)} %bitcast.106, f32[1024,768]{0,1:T(8,128)S(1)} %get-tuple-element.242, f32[768]{0:T(1024)S(1)} %get-tuple-element.179, f32[768]{0:T(1024)S(1)} %get-tuple-element.180, f32[1024]{0:T(1024)S(1)} %add_rsqrt_fusion.1, f32[1024]{0:T(1024)S(1)} %broadcast_multiply_fusion.10), kind=kOutput, calls=%fused_computation.193 | convolution fusion | flops 4835770368 | bytes 20461568 | tf_op jit(solution)/shard_map/dot_general | solution.py:53
  158.3 11.5 %fusion.80 = (f32[1024]{0:T(1024)S(1)}, f32[1024,768]{0,1:T(8,128)S(1)}) fusion(f32[1024,768]{0,1:T(8,128)S(1)} %get-tuple-element.242, bf16[768,3072]{1,0:T(8,128)(2,1)} %get-tuple-element.75, f32[1024,3072]{1,0:T(8,128)S(1)} %fusion.61), kind=kOutput, calls=%fused_computation.198 | convolution fusion | flops 4861721600 | bytes 23597056 | tf_op jit(solution)/shard_map/dot_general | solution.py:53
  172.8 1.3 fusion.43
  174.2 2.8 fusion.83
  177.0 3.5 copy.134
  180.5 4.0 multiply_reduce_fusion
  186.0 18.1 %fusion.6 = bf16[1024,3072]{1,0:T(8,128)(2,1)S(1)} fusion(f32[1024,3072]{1,0:T(8,128)} %copy-done.12, bf16[768,3072]{1,0:T(8,128)(2,1)} %get-tuple-element.75, f32[1024,768]{0,1:T(8,128)S(1)} %subtract_multiply_fusion), kind=kOutput, calls=%fused_computation.8 | convolution fusion | flops 4895539200 | bytes 26738688 | tf_op jit(solution)/shard_map/dot_general | solution.py:53
  204.2 6.8 %fusion.82 = (f32[768]{0:T(1024)S(1)}, f32[1024,768]{1,0:T(8,128)}) fusion(bf16[1024,3072]{1,0:T(8,128)(2,1)S(1)} %fusion.6, bf16[768,3072]{1,0:T(8,128)(2,1)S(1)} %bitcast.108), kind=kOutput, calls=%fused_computation.200 | convolution fusion | flops 4832623616 | bytes 14158848 | tf_op jit(solution)/shard_map/dot_general | solution.py:53
  211.0 3.7 copy.135
  214.7 4.0 multiply_reduce_fusion.1
  219.4 3.2 fusion.75
  222.6 2.6 convolution_convert_fusion.4.do_ref
  225.3 37.9 %shard_map.459 = (bf16[1024,768]{1,0:T(8,128)(2,1)S(1)}, bf16[1024,768]{1,0:T(8,128)(2,1)S(1)}, bf16[1024,768]{1,0:T(8,128)(2,1)S(1)}) custom-call(bf16[1024,2304]{1,0:T(8,128)(2,1)} %convolution_convert_fusion.q_ref.k_ref.v_ref, bf16[1024,2304]{1,0:T(8,128)(2,1)} %convolution_convert_fusion.q_ref.k_ref.v_ref, ...), custom_call_target="tpu_custom_call" | custom-call | flops 40000000000 | bytes 12000000 | tf_op jit(solution)/shard_map/pallas_call | solution.py:483
  263.5 1.8 copy-done.67
  265.3 5.6 %fusion.81 = (f32[768]{0:T(1024)S(1)}, f32[1024,768]{1,0:T(8,128)}) fusion(bf16[1024,2304]{1,0:T(8,128)(2,1)S(1)} %constant_dynamic-update-slice_fusion, bf16[768,2304]{1,0:T(8,128)(2,1)S(1)} %copy-done.67), kind=kOutput, calls=%fused_computation.199 | convolution fusion | flops 3624664320 | bytes 11406336 | tf_op jit(solution)/shard_map/dot_general | solution.py:53
  270.9 3.7 copy.137
  274.6 3.2 multiply_reduce_fusion.2
  278.4 1.6 fusion.76
  280.0 2.0 fusion.15
  282.1 3.6 fusion.9
  285.8 6.0 %convolution_convert_fusion.3 = bf16[768,2304]{1,0:T(8,128)(2,1)} fusion(bf16[1024,2304]{1,0:T(8,128)(2,1)S(1)} %bitcast.118, f32[768]{0:T(1024)S(1)} %copy-done.63, f32[768]{0:T(1024)S(1)} %copy-done.52, f32[1024]{0:T(1024)S(1)} %copy-done.54, f32[1024]{0:T(1024)S(1)} %copy-done.49, f32[1024,768]{0,1:T(8,128)S(1)} %copy-done.10, ...), kind=kOutput, calls=%fused_computation.13 | convolution fusion | flops 3630366720 | bytes 11420672 | tf_op jit(solution)/shard_map/dot_general | solution.py:53
  291.8 2.5 convolution_convert_fusion.5
  294.3 7.1 %convolution_convert_fusion.1 = bf16[768,3072]{1,0:T(8,128)(2,1)} fusion(bf16[1024,3072]{1,0:T(8,128)(2,1)S(1)} %bitcast.135, f32[1024,768]{0,1:T(8,128)S(1)} %copy-done.4, f32[768]{0:T(1024)S(1)} %get-tuple-element.179, f32[768]{0:T(1024)S(1)} %get-tuple-element.180, f32[1024]{0:T(1024)S(1)} %add_rsqrt_fusion.1, f32[1024]{0:T(1024)S(1)} %broadcast_multiply_fusion.10), kind=kOutput, calls=%fused_computation.11 | convolution fusion | flops 4838129664 | bytes 14170112 | tf_op jit(solution)/shard_map/dot_general | solution.py:53
  301.5 7.1 %convolution_convert_fusion.2 = bf16[768,3072]{1,0:T(8,128)(2,1)} fusion(f32[1024,768]{0,1:T(8,128)S(1)} %copy-done.14, f32[1024,3072]{1,0:T(8,128)S(1)} %bitcast.103), kind=kOutput, calls=%fused_computation.12 | convolution fusion | flops 4863295488 | bytes 20447232 | tf_op jit(solution)/shard_map/dot_general | solution.py:53
  308.8 1.1 copy.143
  310.0 1.6 copy.139
  313.6 117.8 %shard_map.460 = (f32[96,3072]{1,0:T(8,128)}, f32[96,3072]{1,0:T(8,128)}, f32[96,768]{1,0:T(8,128)}, f32[96,2304]{1,0:T(8,128)}, f32[96,1024]{1,0:T(8,128)}, /*index=5*/f32[96,256]{1,0:T(8,128)}, f32[3,8,128]{2,1,0:T(8,128)}) custom-call(bf16[4,2,2,48,3072]{4,3,2,1,0:T(8,128)(2,1)} %bitcast.110, bf16[4,2,2,48,3072]{4,3,2,1,0:T(8,128)(2,1)} %bitcast.109, ...), custom_call_target="tpu_custom_call" | custom-call | tf_op jit(solution)/shard_map/pallas_call | solution.py:378
  431.4 1.3 slice_reduce_fusion.3
  434.1 2.3 sqrt_add_fusion
  436.4 0.9 copy.152
  437.2 0.9 copy.153
  438.8 1.4 sub.154
  440.3 1.5 copy.157
  441.7 1.5 copy.159
  443.2 1.5 copy.161
  444.7 2.2 multiply_subtract_fusion.6
  446.9 1.5 copy.156
  448.3 1.5 copy.158
  449.8 1.5 copy.160
  451.3 2.2 multiply_subtract_fusion.5
  454.2 4.9 %multiply_subtract_fusion = (f32[3072,96]{0,1:T(8,128)}, f32[3072,96]{0,1:T(8,128)}, f32[3072,96]{0,1:T(8,128)}) fusion(f32[3072,96]{0,1:T(8,128)S(1)} %copy-done.17, f32[]{:T(128)S(6)} %min.3, f32[96,3072]{1,0:T(8,128)} %get-tuple-element.86, f32[]{:T(128)} %get-tuple-element.186, f32[3072,96]{0,1:T(8,128)S(1)} %copy-done.27, f32[3072,96]{0,1:T(8,128)S(1)} %copy-done.28), kind=kLoop, calls=%fused_computation.60 | loop fusion | flops 5013504 | bytes 8257544 | tf_op jit(solution)/shard_map/sub | solution.py:539
  459.2 3.2 multiply_subtract_fusion.1
  462.5 1.7 multiply_subtract_fusion.4
  464.2 2.7 multiply_subtract_fusion.2
  466.9 1.9 multiply_subtract_fusion.3
  (254 shorter events, 23.2 us)
Async XLA Ops:
  0.7 11.2 %copy-start.19 = (f32[96,2304]{1,0:T(8,128)S(1)}, f32[96,2304]{1,0:T(8,128)}, u32[]{:S(2)}) copy-start(f32[96,2304]{1,0:T(8,128)} %param.34) | copy-start | bytes 2654212
  0.7 12.0 %copy-start.24 = (f32[1024,96]{0,1:T(8,128)S(1)}, f32[1024,96]{0,1:T(8,128)}, u32[]{:S(2)}) copy-start(f32[1024,96]{0,1:T(8,128)} %param.33) | copy-start | bytes 1179652
  0.7 12.7 %copy-start.47 = (f32[48,96]{1,0:T(8,128)S(1)}, f32[48,96]{1,0:T(8,128)}, u32[]{:S(2)}) copy-start(f32[48,96]{1,0:T(8,128)} %param.32) | copy-start | bytes 55300
  0.7 12.8 %copy-start.55 = (f32[8,96]{1,0:T(8,128)S(1)}, f32[8,96]{1,0:T(8,128)}, u32[]{:S(2)}) copy-start(f32[8,96]{1,0:T(8,128)} %param.39) | copy-start | bytes 9220
  0.7 12.9 %copy-start.46 = (f32[96,96]{1,0:T(8,128)S(1)}, f32[96,96]{1,0:T(8,128)}, u32[]{:S(2)}) copy-start(f32[96,96]{1,0:T(8,128)} %param.38) | copy-start | bytes 110596
  0.7 12.9 %copy-start.32 = (f32[96,768]{1,0:T(8,128)S(1)}, f32[96,768]{1,0:T(8,128)}, u32[]{:S(2)}) copy-start(f32[96,768]{1,0:T(8,128)} %param.35) | copy-start | bytes 884740
  1.6 98.1 %collective-permute-start = (s32[256]{0:T(256)S(1)}, s32[256]{0:T(256)S(1)}, u32[]{:S(2)}, u32[]{:S(2)}) collective-permute-start(s32[256]{0:T(256)S(1)} %bitcast.133), channel_id=1, source_target_pairs={{0,1},{1,0},{2,3},{3,2},{4,5},{5,4},{6,7},{7,6},{8,9},{9,8},{10,11... | collective-permute-start | bytes 3080 | tf_op jit(solution)/shard_map/ppermute | solution.py:572
  2.0 99.4 %collective-permute-start.1 = (s32[256]{0:T(256)S(1)}, s32[256]{0:T(256)S(1)}, u32[]{:S(2)}, u32[]{:S(2)}) collective-permute-start(s32[256]{0:T(256)S(1)} %bitcast.129), channel_id=1, source_target_pairs={{0,2},{1,3},{2,0},{3,1},{4,6},{5,7},{6,4},{7,5},{8,10},{9,11},{10,... | collective-permute-start | bytes 3080 | tf_op jit(solution)/shard_map/ppermute | solution.py:572
  4.6 96.9 %collective-permute-start.2 = (s32[256]{0:T(256)S(1)}, s32[256]{0:T(256)S(1)}, u32[]{:S(2)}, u32[]{:S(2)}) collective-permute-start(s32[256]{0:T(256)S(1)} %bitcast.128), channel_id=1, source_target_pairs={{0,3},{1,2},{2,1},{3,0},{4,7},{5,6},{6,5},{7,4},{8,11},{9,10},{10,... | collective-permute-start | bytes 3080 | tf_op jit(solution)/shard_map/ppermute | solution.py:572
  5.5 104.9 %collective-permute-start.3 = (bf16[48,256]{1,0:T(8,128)(2,1)S(1)}, bf16[48,256]{1,0:T(8,128)(2,1)}, u32[]{:S(2)}, u32[]{:S(2)}) collective-permute-start(bf16[48,256]{1,0:T(8,128)(2,1)S(1)} %get-tuple-element.231), channel_id=1, source_target_pairs={{0,1},{1,0},{2,3},{3,2},{4,5},{5,4},{6,7},{7,6},{8,9},{9,8},{10,11... | collective-permute-start | bytes 73736 | tf_op jit(solution)/shard_map/ppermute | solution.py:571
  5.7 105.6 %collective-permute-start.4 = (bf16[48,256]{1,0:T(8,128)(2,1)S(1)}, bf16[48,256]{1,0:T(8,128)(2,1)S(1)}, u32[]{:S(2)}, u32[]{:S(2)}) collective-permute-start(bf16[48,256]{1,0:T(8,128)(2,1)S(1)} %get-tuple-element.233), channel_id=1, source_target_pairs={{0,2},{1,3},{2,0},{3,1},{4,6},{5,7},{6,4},{7,5},{8,10},{9,11},{10,... | collective-permute-start | bytes 73736 | tf_op jit(solution)/shard_map/ppermute | solution.py:571
  9.7 82.8 %copy-start.64 = (f32[8,96]{1,0:T(8,128)S(1)}, f32[8,96]{1,0:T(8,128)}, u32[]{:S(2)}) copy-start(f32[8,96]{1,0:T(8,128)} %param.47) | copy-start | bytes 9220
  9.7 82.8 %copy-start.65 = (f32[8,96]{1,0:T(8,128)S(1)}, f32[8,96]{1,0:T(8,128)}, u32[]{:S(2)}) copy-start(f32[8,96]{1,0:T(8,128)} %param.55) | copy-start | bytes 9220
  15.1 82.0 %copy-start.57 = (f32[48,96]{1,0:T(8,128)S(1)}, f32[48,96]{1,0:T(8,128)}, u32[]{:S(2)}) copy-start(f32[48,96]{1,0:T(8,128)} %param.40) | copy-start | bytes 55300
  15.1 82.7 %copy-start.58 = (f32[48,96]{1,0:T(8,128)S(1)}, f32[48,96]{1,0:T(8,128)}, u32[]{:S(2)}) copy-start(f32[48,96]{1,0:T(8,128)} %param.48) | copy-start | bytes 55300
  94.1 26.7 %copy-start.51 = (f32[768]{0:T(1024)}, f32[768]{0:T(1024)S(1)}, u32[]{:S(2)}) copy-start(f32[768]{0:T(1024)S(1)} %get-tuple-element.183) | copy-start | bytes 9220
  94.1 26.7 %copy-start.62 = (f32[768]{0:T(1024)}, f32[768]{0:T(1024)S(1)}, u32[]{:S(2)}) copy-start(f32[768]{0:T(1024)S(1)} %get-tuple-element.182) | copy-start | bytes 9220
  99.7 11.6 %collective-permute-start.5 = (bf16[48,256]{1,0:T(8,128)(2,1)S(1)}, bf16[48,256]{1,0:T(8,128)(2,1)}, u32[]{:S(2)}, u32[]{:S(2)}) collective-permute-start(bf16[48,256]{1,0:T(8,128)(2,1)S(1)} %get-tuple-element.230), channel_id=1, source_target_pairs={{0,3},{1,2},{2,1},{3,0},{4,7},{5,6},{6,5},{7,4},{8,11},{9,10},{10,... | collective-permute-start | bytes 73736 | tf_op jit(solution)/shard_map/ppermute | solution.py:571
  105.7 5.5 %copy-start.59 = (s32[1024]{0:T(1024)}, s32[1024]{0:T(1024)S(1)}, u32[]{:S(2)}) copy-start(s32[1024]{0:T(1024)S(1)} %select_subtract_fusion) | copy-start | bytes 12292
  106.1 14.2 %copy-start.21 = (bf16[1024,1024]{1,0:T(8,128)(2,1)}, bf16[1024,1024]{1,0:T(8,128)(2,1)S(1)}, u32[]{:S(2)}) copy-start(bf16[1024,1024]{1,0:T(8,128)(2,1)S(1)} %fusion.8) | copy-start | bytes 6291460
  116.4 4.5 copy-start.66
  120.3 29.3 %copy-start.9 = (f32[1024,768]{0,1:T(8,128)}, f32[1024,768]{0,1:T(8,128)S(1)}, u32[]{:S(2)}) copy-start(f32[1024,768]{0,1:T(8,128)S(1)} %get-tuple-element.240) | copy-start | bytes 9437188
  120.3 6.6 %copy-start.48 = (f32[1024]{0:T(1024)}, f32[1024]{0:T(1024)S(1)}, u32[]{:S(2)}) copy-start(f32[1024]{0:T(1024)S(1)} %broadcast_multiply_fusion.11) | copy-start | bytes 12292
  120.8 6.1 %copy-start.53 = (f32[1024]{0:T(1024)}, f32[1024]{0:T(1024)S(1)}, u32[]{:S(2)}) copy-start(f32[1024]{0:T(1024)S(1)} %add_rsqrt_fusion.2) | copy-start | bytes 12292
  127.0 22.7 %copy-start.68 = (bf16[768,768]{1,0:T(8,128)(2,1)S(1)}, bf16[768,768]{1,0:T(8,128)(2,1)}, u32[]{:S(2)}) copy-start(bf16[768,768]{1,0:T(8,128)(2,1)} %get-tuple-element.73) | copy-start | bytes 3538948
  151.4 6.9 %copy-start.2 = (f32[1024,768]{0,1:T(8,128)}, f32[1024,768]{0,1:T(8,128)S(1)}, u32[]{:S(2)}) copy-start(f32[1024,768]{0,1:T(8,128)S(1)} %get-tuple-element.242) | copy-start | bytes 9437188
  158.3 11.6 %copy-start.12 = (f32[1024,3072]{1,0:T(8,128)}, f32[1024,3072]{1,0:T(8,128)S(1)}, u32[]{:S(2)}) copy-start(f32[1024,3072]{1,0:T(8,128)S(1)} %fusion.61) | copy-start | bytes 37748740
  180.5 4.0 copy-start.6
  180.5 4.7 copy-start.7
  185.2 19.0 %slice-start.5 = ((s8[4718592]{0:T(1024)(128)(4,1)}), s8[4194304]{0:T(1024)(128)(4,1)S(1)}, s32[]{:S(2)}) async-start(s8[4718592]{0:T(1024)(128)(4,1)} %bitcast.107), calls=%async_computation.5 | async-start | bytes 8388608
  186.0 18.2 %copy-start.13 = (f32[1024,768]{0,1:T(8,128)}, f32[1024,768]{0,1:T(8,128)S(1)}, u32[]{:S(2)}) copy-start(f32[1024,768]{0,1:T(8,128)S(1)} %subtract_multiply_fusion) | copy-start | bytes 9437188
  186.0 18.2 %slice-start.6 = ((s8[4718592]{0:T(1024)(128)(4,1)}), s8[524288]{0:T(1024)(128)(4,1)S(1)}, s32[]{:S(2)}) async-start(s8[4718592]{0:T(1024)(128)(4,1)} %bitcast.107), calls=%async_computation.6 | async-start | bytes 1048576
  204.2 6.8 %copy-start.69 = (bf16[1024,3072]{1,0:T(8,128)(2,1)}, bf16[1024,3072]{1,0:T(8,128)(2,1)S(1)}, u32[]{:S(2)}) copy-start(bf16[1024,3072]{1,0:T(8,128)(2,1)S(1)} %fusion.6) | copy-start | bytes 18874372
  214.7 4.0 copy-start.3
  214.7 4.7 copy-start.8
  265.3 5.6 %copy-start.38 = (bf16[1024,2304]{1,0:T(8,128)(2,1)}, bf16[1024,2304]{1,0:T(8,128)(2,1)S(1)}, u32[]{:S(2)}) copy-start(bf16[1024,2304]{1,0:T(8,128)(2,1)S(1)} %constant_dynamic-update-slice_fusion) | copy-start | bytes 14155780
  270.8 3.8 copy-start.10
  270.8 3.8 copy-start.49
  270.8 3.8 copy-start.52
  270.9 3.8 copy-start.54
  274.6 3.8 copy-start.16
  280.0 5.7 %slice-start.7 = ((s8[4718592]{0:T(1024)(128)(4,1)}), s8[524288]{0:T(1024)(128)(4,1)S(1)}, s32[]{:S(2)}) async-start(s8[4718592]{0:T(1024)(128)(4,1)} %bitcast.117), calls=%async_computation.7 | async-start | bytes 1048576
  282.1 3.7 slice-start.8
  282.1 12.2 %slice-start.9 = ((s8[6291456]{0:T(1024)(128)(4,1)}), s8[4194304]{0:T(1024)(128)(4,1)S(1)}, s32[]{:S(2)}) async-start(s8[6291456]{0:T(1024)(128)(4,1)} %bitcast.134), calls=%async_computation.9 | async-start | bytes 8388608
  285.8 6.0 %copy-start.1 = (bf16[1024,768]{1,0:T(8,128)(2,1)S(1)}, bf16[1024,768]{1,0:T(8,128)(2,1)}, u32[]{:S(2)}) copy-start(bf16[1024,768]{1,0:T(8,128)(2,1)} %copy-done) | copy-start | bytes 4718596
  285.8 8.5 %slice-start.10 = ((s8[6291456]{0:T(1024)(128)(4,1)}), s8[2097152]{0:T(1024)(128)(4,1)S(1)}, s32[]{:S(2)}) async-start(s8[6291456]{0:T(1024)(128)(4,1)} %bitcast.134), calls=%async_computation.10 | async-start | bytes 4194304
  291.8 9.7 %slice-start = ((s8[12582912]{0:T(1024)(128)(4,1)}), s8[4194304]{0:T(1024)(128)(4,1)S(1)}, s32[]{:S(2)}) async-start(s8[12582912]{0:T(1024)(128)(4,1)} %bitcast.102), calls=%async_computation | async-start | bytes 8388608
  291.8 9.6 %slice-start.1 = ((s8[12582912]{0:T(1024)(128)(4,1)}), s8[4194304]{0:T(1024)(128)(4,1)S(1)}, s32[]{:S(2)}) async-start(s8[12582912]{0:T(1024)(128)(4,1)} %bitcast.102), calls=%async_computation.1 | async-start | bytes 8388608
  294.3 7.1 %slice-start.2 = ((s8[12582912]{0:T(1024)(128)(4,1)}), s8[4194304]{0:T(1024)(128)(4,1)S(1)}, s32[]{:S(2)}) async-start(s8[12582912]{0:T(1024)(128)(4,1)} %bitcast.102), calls=%async_computation.2 | async-start | bytes 8388608
  294.3 7.1 %copy-start.14 = (f32[1024,768]{0,1:T(8,128)S(1)}, f32[1024,768]{0,1:T(8,128)}, u32[]{:S(2)}) copy-start(f32[1024,768]{0,1:T(8,128)} %copy-done.13) | copy-start | bytes 9437188
  301.5 7.2 %copy-start.61 = (f32[768]{0:T(1024)S(1)}, f32[768]{0:T(1024)}, u32[]{:S(2)}) copy-start(f32[768]{0:T(1024)} %get-tuple-element.249) | copy-start | bytes 9220
  301.5 7.2 %copy-start.34 = (f32[768,96]{0,1:T(8,128)S(1)}, f32[768,96]{0,1:T(8,128)}, u32[]{:S(2)}) copy-start(f32[768,96]{0,1:T(8,128)} %fusion.43) | copy-start | bytes 884740
  313.6 124.5 %copy-start.56 = (f32[8,96]{1,0:T(8,128)S(1)}, f32[8,96]{1,0:T(8,128)}, u32[]{:S(2)}) copy-start(f32[8,96]{1,0:T(8,128)} %param.39) | copy-start | bytes 9220
  313.6 140.6 %copy-start.17 = (f32[3072,96]{0,1:T(8,128)S(1)}, f32[3072,96]{0,1:T(8,128)}, u32[]{:S(2)}) copy-start(f32[3072,96]{0,1:T(8,128)} %param.37) | copy-start | bytes 3538948
  313.6 140.6 %copy-start.27 = (f32[3072,96]{0,1:T(8,128)S(1)}, f32[3072,96]{0,1:T(8,128)}, u32[]{:S(2)}) copy-start(f32[3072,96]{0,1:T(8,128)} %param.45) | copy-start | bytes 3538948
  313.6 140.6 %copy-start.28 = (f32[3072,96]{0,1:T(8,128)S(1)}, f32[3072,96]{0,1:T(8,128)}, u32[]{:S(2)}) copy-start(f32[3072,96]{0,1:T(8,128)} %param.53) | copy-start | bytes 3538948
  454.2 4.9 %copy-start.18 = (f32[96,3072]{1,0:T(8,128)S(1)}, f32[96,3072]{1,0:T(8,128)}, u32[]{:S(2)}) copy-start(f32[96,3072]{1,0:T(8,128)} %param.36) | copy-start | bytes 3538948
  454.2 4.9 %copy-start.29 = (f32[96,3072]{1,0:T(8,128)S(1)}, f32[96,3072]{1,0:T(8,128)}, u32[]{:S(2)}) copy-start(f32[96,3072]{1,0:T(8,128)} %param.44) | copy-start | bytes 3538948
  454.2 4.9 %copy-start.30 = (f32[96,3072]{1,0:T(8,128)S(1)}, f32[96,3072]{1,0:T(8,128)}, u32[]{:S(2)}) copy-start(f32[96,3072]{1,0:T(8,128)} %param.52) | copy-start | bytes 3538948
  454.2 4.9 %copy-start.31 = (f32[96,3072]{1,0:T(8,128)S(1)}, f32[96,3072]{1,0:T(8,128)}, u32[]{:S(2)}) copy-start(f32[96,3072]{1,0:T(8,128)} %get-tuple-element.85) | copy-start | bytes 3538948
  459.2 5.0 %copy-start.20 = (f32[96,2304]{1,0:T(8,128)S(1)}, f32[96,2304]{1,0:T(8,128)}, u32[]{:S(2)}) copy-start(f32[96,2304]{1,0:T(8,128)} %param.34) | copy-start | bytes 2654212
  459.2 5.0 %copy-start.35 = (f32[96,2304]{1,0:T(8,128)S(1)}, f32[96,2304]{1,0:T(8,128)}, u32[]{:S(2)}) copy-start(f32[96,2304]{1,0:T(8,128)} %param.42) | copy-start | bytes 2654212
  459.2 5.0 %copy-start.36 = (f32[96,2304]{1,0:T(8,128)S(1)}, f32[96,2304]{1,0:T(8,128)}, u32[]{:S(2)}) copy-start(f32[96,2304]{1,0:T(8,128)} %param.50) | copy-start | bytes 2654212
  459.2 5.0 %copy-start.37 = (f32[96,2304]{1,0:T(8,128)S(1)}, f32[96,2304]{1,0:T(8,128)}, u32[]{:S(2)}) copy-start(f32[96,2304]{1,0:T(8,128)} %get-tuple-element.83) | copy-start | bytes 2654212
  (23 other events, 57.9 us)
